TPU v7x, 32 devices: a whole 2x2x4 slice. The times are simulated.
32 devices in a mesh: dp: 16 (over z, y, core), basis: 2 (over x).
Axes of the slice: x: 2, y: 2, z: 4, core: 2. Of those that a mesh axis runs over, the one named last changes fastest.
Arguments:
- tokens: bfloat16 [32, 640, 768], P(('dp', 'basis')), may hold values from -6 to 6
- w_qkv: bfloat16 [768, 2304], replicated, may hold values from -0.21875 to 0.21875
- w_out: bfloat16 [768, 768], replicated, may hold values from -0.875 to 0.875
- w_up: bfloat16 [768, 3072], replicated, may hold values from -0.21875 to 0.21875
- w_down: bfloat16 [3072, 768], replicated, may hold values from -0.109375 to 0.109375
- gain_one: float32 [768], replicated, may hold values from 0.5 to 1.5
- shift_one: float32 [768], replicated, may hold values from -3 to 3
- gain_two: float32 [768], replicated, may hold values from 0.5 to 1.5
- shift_two: float32 [768], replicated, may hold values from -3 to 3
- coeffs: bfloat16 [32, 256, 768], P('dp', 'basis'), may hold values from -6 to 6
- flags: int32 [32], P(('dp', 'basis')), may hold values 0 or 1
- centres: int32 [32, 12, 2], P('dp'), may hold values from 0 to 255
- widths: int32 [32, 12, 2], P('dp'), may hold values from 1 to 8
- cotangent: bfloat16 [32, 640, 768], P(('dp', 'basis')), may hold values from -6 to 6
Outputs:
- mixed: bfloat16 [32, 640, 768], P(('dp', 'basis'))
- grad_tokens: float32 [32, 640, 768], P(('dp', 'basis'))
- grad_coeffs: float32 [32, 256, 768], P('dp', 'basis')
- grad_w_qkv: float32 [768, 2304], P(('dp', 'basis'))
- grad_w_out: float32 [768, 768], P(('dp', 'basis'))
- grad_w_up: float32 [768, 3072], P(('dp', 'basis'))
- grad_w_down: float32 [3072, 768], P(('dp', 'basis'))
- grad_gain_one: float32 [768], P(('dp', 'basis'))
- grad_shift_one: float32 [768], P(('dp', 'basis'))
- grad_gain_two: float32 [768], P(('dp', 'basis'))
- grad_shift_two: float32 [768], P(('dp', 'basis'))
Inputs may be any that keep to these rules, and one draw needn't show every extreme that they name: `flags`: 1 where a sequence carries memory coefficients, 0 where its memory is empty.
All inputs are finite; a program needn't handle non-finite values. No bound on the sum of `flags` on one device may be relied on, other than what follows from the above.
Results may differ from a plain program's by a relative error of at most 0.014.
Values may be sent and summed in bfloat16 or wider, within the bound.
A program may use at most 256 MiB of HBM per device.

v0:
```python
import math

import jax
import jax.numpy as jnp
from jax import lax
from jax.sharding import PartitionSpec as P

eps = 1e-05


def norm_parts(values, gain, shift):
    centred = values - jnp.mean(values, axis=-1, keepdims=True)
    inverse = lax.rsqrt(jnp.mean(centred * centred, axis=-1, keepdims=True) + eps)
    normed = centred * inverse
    return (normed * gain + shift, normed, inverse)


def norm_back(upstream, normed, inverse, gain):
    scaled = upstream * gain
    inner = (
        scaled
        - jnp.mean(scaled, axis=-1, keepdims=True)
        - normed * jnp.mean(scaled * normed, axis=-1, keepdims=True)
    )
    return (inverse * inner, jnp.sum(upstream * normed, axis=0), jnp.sum(upstream, axis=0))


def basis_weights(centres, widths, rows):
    spread = (widths * widths).astype(jnp.float32) + 4.0
    gap = centres[..., None].astype(jnp.float32) - rows.astype(jnp.float32)
    return 2.0 * lax.rsqrt(spread)[..., None] * jnp.exp(-gap * gap / (2.0 * spread[..., None]))


def causal_scores(query_part, key_part, first, scale):
    scores = (
        jnp.einsum("qhe,khe->hqk", query_part, key_part, preferred_element_type=jnp.float32) * scale
    )
    row_ids = first + jnp.arange(query_part.shape[0], dtype=jnp.int32)[:, None]
    col_ids = jnp.arange(key_part.shape[0], dtype=jnp.int32)[None, :]
    return jnp.where(col_ids <= row_ids, scores, -1e30)


def on_device(
    tokens,
    w_qkv,
    w_out,
    w_up,
    w_down,
    gain_one,
    shift_one,
    gain_two,
    shift_two,
    coeffs,
    flags,
    centres,
    widths,
    cotangent,
):
    seq_len, width = (tokens.shape[1], tokens.shape[2])
    heads, blocks = (centres.shape[1], centres.shape[2])
    head_dim = width // heads
    span = seq_len // blocks
    scale = 1.0 / math.sqrt(head_dim)
    local_rows = coeffs.shape[1]
    step = min(512, seq_len)
    starts = list(range(0, seq_len, step))
    resid = tokens[0].astype(jnp.float32)
    normed_in, normed_one, inverse_one = norm_parts(resid, gain_one, shift_one)
    hidden_one = normed_in.astype(jnp.bfloat16)
    qkv = jnp.dot(hidden_one, w_qkv, preferred_element_type=jnp.float32).astype(jnp.bfloat16)
    qkv = qkv.reshape(seq_len, 3, heads, head_dim)
    query, key, value = (qkv[:, 0], qkv[:, 1], qkv[:, 2])
    rows = lax.axis_index("basis") * local_rows + jnp.arange(local_rows, dtype=jnp.int32)
    weights_e = basis_weights(centres, widths, rows).astype(jnp.bfloat16)
    partial_mem = jnp.einsum(
        "shbj,sjd->shbd", weights_e, coeffs, preferred_element_type=jnp.float32
    )
    summed = lax.psum_scatter(
        partial_mem.astype(jnp.bfloat16), "basis", scatter_dimension=0, tiled=True
    ).astype(jnp.float32)
    memory = summed[0].astype(jnp.bfloat16)
    local_parts = []
    log_totals = []
    for first in starts:
        finish = min(first + step, seq_len)
        scores = causal_scores(query[first:finish], key[:finish], first, scale)
        peak = jnp.max(scores, axis=-1, keepdims=True)
        expo = jnp.exp(scores - peak)
        total = jnp.sum(expo, axis=-1, keepdims=True)
        probs = (expo / total).astype(jnp.bfloat16)
        log_totals.append(peak + jnp.log(total))
        local_parts.append(
            jnp.einsum("hqk,khe->qhe", probs, value[:finish], preferred_element_type=jnp.float32)
        )
    local = jnp.concatenate(local_parts, axis=0)
    w_kv = w_qkv[:, width:].reshape(width, 2, heads, head_dim)
    mem_kv = jnp.einsum("hbd,dche->chbe", memory, w_kv, preferred_element_type=jnp.float32).astype(
        jnp.bfloat16
    )
    mem_key, mem_value = (mem_kv[0], mem_kv[1])
    flag = flags[0].astype(jnp.float32)
    query_blocks = query.reshape(blocks, span, heads, head_dim)
    mem_score = (
        jnp.einsum("bthe,hbe->bth", query_blocks, mem_key, preferred_element_type=jnp.float32)
        * scale
    )
    sigma = jax.nn.sigmoid(mem_score)
    gate = sigma * flag
    long_term = gate[..., None] * jnp.transpose(mem_value, (1, 0, 2))[:, None].astype(jnp.float32)
    attended = local + long_term.reshape(seq_len, heads, head_dim)
    joined = attended.reshape(seq_len, width).astype(jnp.bfloat16)
    after = resid + jnp.dot(joined, w_out, preferred_element_type=jnp.float32)
    normed_mid, normed_two, inverse_two = norm_parts(after, gain_two, shift_two)
    hidden_two = normed_mid.astype(jnp.bfloat16)
    pre = jnp.dot(hidden_two, w_up, preferred_element_type=jnp.float32)
    act_value, gelu_back = jax.vjp(lambda inner: jax.nn.gelu(inner, approximate=True), pre)
    act = act_value.astype(jnp.bfloat16)
    final = after + jnp.dot(act, w_down, preferred_element_type=jnp.float32)
    mixed = final.astype(jnp.bfloat16)[None]
    grad_final = cotangent[0].astype(jnp.float32)
    grad_mlp = cotangent[0]
    grad_w_down = jnp.dot(act.T, grad_mlp, preferred_element_type=jnp.float32)
    grad_act = jnp.dot(grad_mlp, w_down.T, preferred_element_type=jnp.float32)
    grad_pre = gelu_back(grad_act)[0].astype(jnp.bfloat16)
    grad_w_up = jnp.dot(hidden_two.T, grad_pre, preferred_element_type=jnp.float32)
    grad_hidden_two = jnp.dot(grad_pre, w_up.T, preferred_element_type=jnp.float32)
    grad_after_norm, grad_gain_two, grad_shift_two = norm_back(
        grad_hidden_two, normed_two, inverse_two, gain_two
    )
    grad_after = grad_final + grad_after_norm
    grad_branch = grad_after.astype(jnp.bfloat16)
    grad_w_out = jnp.dot(joined.T, grad_branch, preferred_element_type=jnp.float32)
    grad_heads = jnp.dot(grad_branch, w_out.T, preferred_element_type=jnp.float32).astype(
        jnp.bfloat16
    )
    grad_heads = grad_heads.reshape(seq_len, heads, head_dim)
    grad_blocks = grad_heads.reshape(blocks, span, heads, head_dim)
    grad_gate = (
        jnp.einsum("bthe,hbe->bth", grad_blocks, mem_value, preferred_element_type=jnp.float32)
        * flag
    )
    grad_mem_value = jnp.einsum("bth,bthe->hbe", gate, grad_blocks.astype(jnp.float32))
    grad_score = grad_gate * sigma * (1.0 - sigma) * scale
    grad_query_mem = grad_score[..., None] * jnp.transpose(mem_key, (1, 0, 2))[:, None].astype(
        jnp.float32
    )
    grad_mem_key = jnp.einsum("bth,bthe->hbe", grad_score, query_blocks.astype(jnp.float32))
    grad_mem_kv = jnp.stack([grad_mem_key, grad_mem_value]).astype(jnp.bfloat16)
    grad_w_kv = jnp.einsum(
        "hbd,chbe->dche", memory, grad_mem_kv, preferred_element_type=jnp.float32
    ).reshape(width, 2 * width)
    grad_memory = jnp.einsum(
        "chbe,dche->hbd", grad_mem_kv, w_kv, preferred_element_type=jnp.float32
    ).astype(jnp.bfloat16)
    grad_memory_all = lax.all_gather(grad_memory[None], "basis", axis=0, tiled=True)
    grad_coeffs = jnp.einsum(
        "shbj,shbd->sjd", weights_e, grad_memory_all, preferred_element_type=jnp.float32
    )
    grad_query = grad_query_mem.reshape(seq_len, heads, head_dim)
    grad_key = jnp.zeros((seq_len, heads, head_dim), jnp.float32)
    grad_value = jnp.zeros((seq_len, heads, head_dim), jnp.float32)
    for index, first in enumerate(starts):
        finish = min(first + step, seq_len)
        scores = causal_scores(query[first:finish], key[:finish], first, scale)
        probs_full = jnp.exp(scores - log_totals[index])
        probs = probs_full.astype(jnp.bfloat16)
        upstream = grad_heads[first:finish]
        grad_probs = jnp.einsum(
            "qhe,khe->hqk", upstream, value[:finish], preferred_element_type=jnp.float32
        )
        grad_scores = probs_full * (
            grad_probs - jnp.sum(probs_full * grad_probs, axis=-1, keepdims=True)
        )
        grad_scores = grad_scores.astype(jnp.bfloat16)
        grad_value = grad_value.at[:finish].add(
            jnp.einsum("hqk,qhe->khe", probs, upstream, preferred_element_type=jnp.float32)
        )
        grad_key = grad_key.at[:finish].add(
            jnp.einsum(
                "hqk,qhe->khe", grad_scores, query[first:finish], preferred_element_type=jnp.float32
            )
            * scale
        )
        grad_query = grad_query.at[first:finish].add(
            jnp.einsum(
                "hqk,khe->qhe", grad_scores, key[:finish], preferred_element_type=jnp.float32
            )
            * scale
        )
    grad_qkv = (
        jnp.stack([grad_query, grad_key, grad_value], axis=1)
        .reshape(seq_len, 3 * width)
        .astype(jnp.bfloat16)
    )
    grad_w_qkv = jnp.dot(hidden_one.T, grad_qkv, preferred_element_type=jnp.float32)
    grad_w_qkv = grad_w_qkv.at[:, width:].add(grad_w_kv)
    grad_hidden_one = jnp.dot(grad_qkv, w_qkv.T, preferred_element_type=jnp.float32)
    grad_resid_norm, grad_gain_one, grad_shift_one = norm_back(
        grad_hidden_one, normed_one, inverse_one, gain_one
    )
    grad_tokens = (grad_after + grad_resid_norm)[None]
    small = jnp.stack([grad_gain_one, grad_shift_one, grad_gain_two, grad_shift_two])
    parts = (
        lax.psum_scatter(grad_w_qkv, ("dp", "basis"), scatter_dimension=0, tiled=True),
        lax.psum_scatter(grad_w_out, ("dp", "basis"), scatter_dimension=0, tiled=True),
        lax.psum_scatter(grad_w_up, ("dp", "basis"), scatter_dimension=0, tiled=True),
        lax.psum_scatter(grad_w_down, ("dp", "basis"), scatter_dimension=0, tiled=True),
        lax.psum_scatter(small, ("dp", "basis"), scatter_dimension=1, tiled=True),
    )
    share_qkv, share_out, share_up, share_down, share_small = parts
    return (
        mixed,
        grad_tokens,
        grad_coeffs,
        share_qkv,
        share_out,
        share_up,
        share_down,
        share_small[0],
        share_small[1],
        share_small[2],
        share_small[3],
    )


def solution(mesh):
    in_specs = (
        P(("dp", "basis"), None, None),
        P(),
        P(),
        P(),
        P(),
        P(),
        P(),
        P(),
        P(),
        P("dp", "basis", None),
        P(("dp", "basis")),
        P("dp", None, None),
        P("dp", None, None),
        P(("dp", "basis"), None, None),
    )
    out_specs = (
        P(("dp", "basis"), None, None),
        P(("dp", "basis"), None, None),
        P("dp", "basis", None),
        P(("dp", "basis"), None),
        P(("dp", "basis"), None),
        P(("dp", "basis"), None),
        P(("dp", "basis"), None),
        P(("dp", "basis")),
        P(("dp", "basis")),
        P(("dp", "basis")),
        P(("dp", "basis")),
    )
    return jax.shard_map(
        on_device, mesh=mesh, in_specs=in_specs, out_specs=out_specs, check_vma=False
    )
```

profile of v0, /device:TPU:0, one launch (start us, length us, event | category | flops | bytes accessed | tf_op | source)
XLA Modules:
  0.0 629.1 jit_solution(3998574859957928773)
XLA Ops:
  9.3 1.9 convolution_convert_fusion.2
  11.4 1.5 convert_reduce_fusion
  13.0 1.8 fusion.37
  15.5 4.2 convolution_convert_fusion
  19.7 5.7 copy.80
  25.4 2.2 slice.256
  27.7 3.4 fusion.14
  31.1 2.6 fusion
  33.7 1.3 log_add_fusion
  35.6 5.8 fusion.12
  42.8 2.4 copy.125
  45.2 3.8 reshape_squeeze.3
  49.0 2.1 fusion.133
  51.1 1.1 fusion.15
  52.2 3.2 fusion.48
  56.1 1.8 fusion.77
  58.5 1.0 copy.85
  59.5 1.9 mul.306
  61.4 3.1 mul.307
  64.5 1.7 fusion.66
  67.6 2.6 fusion.44
  70.3 1.1 fusion.134
  71.8 3.4 fusion.131
  75.2 7.4 %fusion.8 = bf16[640,3072]{1,0:T(8,128)(2,1)S(1)} fusion(f32[640,3072]{1,0:T(8,128)S(1)} %fusion.131, bf16[3072,768]{1,0:T(8,128)(2,1)S(1)} %bitcast.288, bf16[1,640,768]{2,1,0:T(8,128)(2,1)S(1)} %copy-done.26), kind=kOutput, calls=%fused_computation.16 | convolution fusion | flops 3059220480 | bytes 17498112 | tf_op jit(solution)/shard_map/dot_general | solution.py:123
  82.7 4.2 multiply_reduce_fusion.2
  87.6 1.0 convolution_convert_fusion.1
  90.5 2.4 copy.86
  92.9 2.5 fusion.101
  95.6 2.0 mul.342
  97.6 3.8 mul.343
  101.6 2.4 copy.88
  104.0 3.8 reshape_reshape.3
  107.8 1.8 fusion.60
  109.6 1.6 fusion.64
  112.8 2.7 copy.96
  115.5 6.1 copy.97
  121.7 11.3 %multiply_reduce_fusion = (f32[12,512]{1,0:T(8,128)S(1)}, f32[12,512,512]{1,2,0:T(8,128)}) fusion(f32[12,512]{1,0:T(8,128)S(1)} %copy-done.29, f32[12,512,512]{1,2,0:T(8,128)} %copy-done.2, pred[512,512]{0,1:T(8,128)(4,1)S(1)} %copy-done.15, bf16[512,12,64]{0,2,1:T(8,128)(2,1)S(1)} %bitcast.268, bf16[640,3,12,64]{0,3,2,1:T(8,128)(2,1)} %bitcast.258), kind=kOutput, calls=%fused_computation.1 | convolution fusion | flops 418375680 | bytes 27049984 | tf_op jit(solution)/shard_map/qhe,khe->hqk/dot_general | solution.py:168
  133.0 1.9 slice-done.2
  134.9 7.2 %multiply_convert_fusion = bf16[12,512,512]{1,2,0:T(8,128)(2,1)S(1)} fusion(f32[12,512,512]{1,2,0:T(8,128)} %get-tuple-element.139, f32[12,512]{1,0:T(8,128)S(1)} %get-tuple-element.138, f32[12,512]{1,0:T(8,128)S(1)} %copy-done.29, f32[12,512,512]{1,2,0:T(8,128)S(1)} %bitcast.252, pred[512,512]{0,1:T(8,128)(4,1)S(1)} %copy-done.15), kind=kLoop, calls=%fused_computation | loop fusion | flops 18874368 | bytes 31768576 | tf_op jit(solution)/shard_map/convert_element_type | solution.py:174
  142.2 2.0 multiply_bitcast_fusion
  144.4 1.1 fusion.51
  145.5 1.3 copy.164
  146.8 1.6 copy-done.4
  148.4 1.5 multiply_reduce_fusion.1
  149.9 1.0 multiply_convert_fusion.2
  150.9 1.5 fusion.46
  152.3 4.1 fusion.52
  156.4 2.5 fusion.45
  158.9 0.9 fusion.59
  160.6 1.6 copy-done.23
  162.2 5.8 fusion.81
  168.1 5.5 fusion.13
  173.6 12.0 %fusion.84 = f32[3072,768]{1,0:T(8,128)} fusion(bf16[1,640,768]{2,1,0:T(8,128)(2,1)} %param.45, f32[640,3072]{1,0:T(8,128)} %copy-done.59), kind=kOutput, calls=%fused_computation.112 | convolution fusion | flops 3037593600 | bytes 18284544 | tf_op jit(solution)/shard_map/dot_general | solution.py:122
  186.4 10.4 %fusion.130 = f32[768,3072]{1,0:T(8,128)} fusion(bf16[640,3072]{1,0:T(8,128)(2,1)} %copy-done.21, f32[640,768]{1,0:T(8,128)} %copy-done.6, f32[768]{0:T(1024)S(1)} %copy-done.35, f32[768]{0:T(1024)S(1)} %copy-done.33, f32[640]{0:T(1024)S(1)} %copy-done.31, f32[640]{0:T(1024)S(1)} %broadcast_multiply_fusion.5), kind=kOutput, calls=%fused_computation.192 | convolution fusion | flops 3022356480 | bytes 15346688 | tf_op jit(solution)/shard_map/dot_general | solution.py:125
  197.5 7.0 %fusion.36 = (f32[768]{0:T(1024)S(1)}, f32[640]{0:T(1024)S(1)}, f32[640]{0:T(1024)S(1)}, f32[768]{0:T(1024)S(1)}, f32[640,768]{1,0:T(8,128)}) fusion(bf16[1,640,768]{2,1,0:T(8,128)(2,1)S(1)} %copy-done.11, f32[640]{0:T(1024)S(1)} %copy-done.44, f32[640]{0:T(1024)S(1)} %copy-done.40, f32[768]{0:T(1024)S(1)} %copy-done.52, bf16[640,2304]{0,1:T(8,128)(2,1)} %bitcast.271, ...), kind=kOutput, calls=%fused_computation.57 | convolution fusion | flops 2269836544 | bytes 9456640 | tf_op jit(solution)/shard_map/dot_general | solution.py:197
  204.5 42.3 %all-reduce.2 = f32[4,768]{1,0:T(4,128)S(1)} all-reduce(f32[4,768]{1,0:T(4,128)S(1)} %pad_maximum_fusion.1), channel_id=8, replica_groups=mesh['dp'=16,'basis'=2] {'dp','basis'}, use_global_device_ids=true, to_apply=%region_23.24.clone | all-reduce | flops 3072 | bytes 24576
  246.8 2.4 fusion.71
  249.2 5.0 all-gather
  254.3 1.3 convolution_bitcast_fusion.1
  256.1 2.0 fusion.35
  258.1 10.6 %fusion.55 = bf16[1,640,768]{2,1,0:T(8,128)(2,1)} fusion(f32[640,768]{1,0:T(8,128)S(1)} %copy-done.7, bf16[3072,768]{1,0:T(8,128)(2,1)} %param.36, f32[640,3072]{1,0:T(8,128)} %copy-done.59), kind=kOutput, calls=%fused_computation.87 | convolution fusion | flops 3038576640 | bytes 15532032 | tf_op jit(solution)/shard_map/dot_general | solution.py:118
  268.7 70.5 %reduce-scatter.9.cloned.1.call-done = f32[24,2304]{1,0:T(8,128)} async-done(((f32[768,2304]{1,0:T(8,128)}), f32[24,2304]{1,0:T(8,128)}) %reduce-scatter.9.cloned.1.call-update) | async-done | bytes 221200 | tf_op jit(solution)/shard_map/reduce_scatter | solution.py:204
  339.2 141.2 %reduce-scatter.15.cloned.1.call-done = f32[96,768]{1,0:T(8,128)} async-done(((f32[3072,768]{1,0:T(8,128)}), f32[96,768]{1,0:T(8,128)}) %reduce-scatter.15.cloned.1.call-update) | async-done | bytes 294928 | tf_op jit(solution)/shard_map/reduce_scatter | solution.py:207
  480.4 141.9 %reduce-scatter.13.cloned.1.call-done = f32[24,3072]{1,0:T(8,128)} async-done(((f32[768,3072]{1,0:T(8,128)}), f32[24,3072]{1,0:T(8,128)}) %reduce-scatter.13.cloned.1.call-update) | async-done | bytes 294928 | tf_op jit(solution)/shard_map/reduce_scatter | solution.py:206
  (193 shorter events, 15.0 us)
Async XLA Ops:
  7.2 63.0 %copy-start = (bf16[768,768]{1,0:T(8,128)(2,1)S(1)}, bf16[768,768]{1,0:T(8,128)(2,1)}, u32[]{:S(2)}) copy-start(bf16[768,768]{1,0:T(8,128)(2,1)} %param.34) | copy-start | bytes 3538948
  7.2 48.9 %reduce-scatter.7.cloned.1.call-start = ((), (), s32[]{:S(2)}) async-start(), calls=%async_computation.5 | async-start | bytes 147456 | tf_op jit(solution)/shard_map/reduce_scatter | solution.py:78
  7.3 1.5 copy-start.55
  11.2 257.4 %reduce-scatter.11.cloned.1.call-start = ((), (), s32[]{:S(2)}) async-start(), calls=%async_computation.7 | async-start | bytes 2433024 | tf_op jit(solution)/shard_map/reduce_scatter | solution.py:205
  11.4 19.7 %copy-start.14 = (pred[512,512]{0,1:T(8,128)(4,1)}, pred[512,512]{0,1:T(8,128)(4,1)S(1)}, u32[]{:S(2)}) copy-start(pred[512,512]{0,1:T(8,128)(4,1)S(1)} %iota_compare_fusion) | copy-start | bytes 786436
  12.9 2.4 copy-start.8
  12.9 2.6 copy-start.9
  12.9 2.5 copy-start.51
  12.9 2.5 copy-start.57
  13.0 1.8 copy-start.39
  31.1 4.5 copy-start.2
  35.6 7.2 %slice-start.5 = ((bf16[768,2304]{1,0:T(8,128)(2,1)}), bf16[768,1536]{1,0:T(8,128)(2,1)S(1)}, s32[]{:S(2)}) async-start(bf16[768,2304]{1,0:T(8,128)(2,1)} %param.33), calls=%async_computation.15 | async-start | bytes 4718592 | tf_op jit(solution)/shard_map/slice | solution.py:96
  51.1 4.3 copy-start.3
  52.2 3.8 copy-start.24
  64.5 5.7 copy-start.10
  67.6 4.2 slice-start.7
  70.2 1.5 copy-start.32
  70.2 1.5 copy-start.34
  70.2 1.6 slice-start.8
  70.2 4.9 slice-start.9
  71.4 15.5 %copy-start.6 = (f32[640,768]{1,0:T(8,128)}, f32[640,768]{1,0:T(8,128)S(1)}, u32[]{:S(2)}) copy-start(f32[640,768]{1,0:T(8,128)S(1)} %get-tuple-element.136) | copy-start | bytes 5898244
  71.8 15.0 %copy-start.30 = (f32[640]{0:T(1024)}, f32[640]{0:T(1024)S(1)}, u32[]{:S(2)}) copy-start(f32[640]{0:T(1024)S(1)} %add_rsqrt_fusion) | copy-start | bytes 7684
  71.8 3.4 copy-start.26
  71.8 3.4 slice-start.10
  75.2 7.4 %copy-start.59 = (f32[640,3072]{1,0:T(8,128)}, f32[640,3072]{1,0:T(8,128)S(1)}, u32[]{:S(2)}) copy-start(f32[640,3072]{1,0:T(8,128)S(1)} %fusion.131) | copy-start | bytes 23592964
  82.7 4.2 copy-start.21
  88.6 4.3 copy-start.18
  92.9 2.5 copy-start.38
  95.6 5.8 slice-start.6
  101.4 8.2 %copy-start.37 = (bf16[12,2,64,1]{2,1,0,3:T(2,128)(2,1)S(1)}, bf16[12,2,64,1]{2,1,0,3:T(2,128)(2,1)}, u32[]{:S(2)}) copy-start(bf16[12,2,64,1]{2,1,0,3:T(2,128)(2,1)} %get-tuple-element.121) | copy-start | bytes 9220
  101.6 6.2 copy-start.42
  101.6 9.6 %copy-start.28 = (f32[2,12,320]{2,0,1:T(2,128)S(1)}, f32[2,12,320]{2,0,1:T(2,128)}, u32[]{:S(2)}) copy-start(f32[2,12,320]{2,0,1:T(2,128)} %copy-done.27) | copy-start | bytes 92164
  101.6 9.6 %copy-start.16 = (bf16[2,320,12,64]{1,0,3,2:T(2,128)(2,1)S(1)}, bf16[2,320,12,64]{1,0,3,2:T(2,128)(2,1)}, u32[]{:S(2)}) copy-start(bf16[2,320,12,64]{1,0,3,2:T(2,128)(2,1)} %reshape_squeeze.3) | copy-start | bytes 2949124
  107.8 4.2 copy-start.41
  111.9 227.3 %reduce-scatter.9.cloned.1.call-start = ((), (), s32[]{:S(2)}) async-start(), calls=%async_computation.6 | async-start | bytes 7299072 | tf_op jit(solution)/shard_map/reduce_scatter | solution.py:204
  115.5 6.2 copy-start.15
  115.5 6.2 copy-start.22
  115.5 6.2 copy-start.29
  121.7 11.3 %slice-start = ((s8[12582912]{0:T(1024)(128)(4,1)}), s8[4194304]{0:T(1024)(128)(4,1)S(1)}, s32[]{:S(2)}) async-start(s8[12582912]{0:T(1024)(128)(4,1)} %bitcast.251), calls=%async_computation.10 | async-start | bytes 8388608
  121.7 11.3 %slice-start.1 = ((s8[12582912]{0:T(1024)(128)(4,1)}), s8[4194304]{0:T(1024)(128)(4,1)S(1)}, s32[]{:S(2)}) async-start(s8[12582912]{0:T(1024)(128)(4,1)} %bitcast.251), calls=%async_computation.11 | async-start | bytes 8388608
  121.7 13.2 %slice-start.2 = ((s8[12582912]{0:T(1024)(128)(4,1)}), s8[4194304]{0:T(1024)(128)(4,1)S(1)}, s32[]{:S(2)}) async-start(s8[12582912]{0:T(1024)(128)(4,1)} %bitcast.251), calls=%async_computation.12 | async-start | bytes 8388608
  134.9 7.3 %copy-start.5 = (bf16[640,2304]{0,1:T(8,128)(2,1)S(1)}, bf16[640,2304]{0,1:T(8,128)(2,1)}, u32[]{:S(2)}) copy-start(bf16[640,2304]{0,1:T(8,128)(2,1)} %copy.80) | copy-start | bytes 8847364
  142.1 2.0 copy-start.12
  144.4 2.4 copy-start.36
  145.5 2.9 copy-start.4
  156.4 2.5 copy-start.13
  158.9 1.2 copy-start.20
  160.1 2.1 copy-start.11
  160.1 2.1 copy-start.40
  160.1 2.1 copy-start.44
  160.1 2.1 copy-start.52
  160.1 2.1 copy-start.58
  160.2 7.9 %slice-start.3 = ((s8[4718592]{0:T(1024)(128)(4,1)}), s8[4194304]{0:T(1024)(128)(4,1)S(1)}, s32[]{:S(2)}) async-start(s8[4718592]{0:T(1024)(128)(4,1)} %bitcast.264), calls=%async_computation.13 | async-start | bytes 8388608
  160.6 1.6 copy-start.23
  162.2 5.8 slice-start.4
  173.6 306.8 %reduce-scatter.15.cloned.1.call-start = ((), (), s32[]{:S(2)}) async-start(), calls=%async_computation.9 | async-start | bytes 9732096 | tf_op jit(solution)/shard_map/reduce_scatter | solution.py:207
  185.7 436.7 %reduce-scatter.13.cloned.1.call-start = ((), (), s32[]{:S(2)}) async-start(), calls=%async_computation.8 | async-start | bytes 9732096 | tf_op jit(solution)/shard_map/reduce_scatter | solution.py:206
  197.5 56.8 %copy-start.46 = (f32[2,12,2]{1,2,0:T(2,128)S(1)}, f32[2,12,2]{1,2,0:T(2,128)}, u32[]{:S(2)}) copy-start(f32[2,12,2]{1,2,0:T(2,128)} %copy-done.45) | copy-start | bytes 580
  197.5 56.8 %copy-start.48 = (f32[2,12,2]{1,2,0:T(2,128)S(1)}, f32[2,12,2]{1,2,0:T(2,128)}, u32[]{:S(2)}) copy-start(f32[2,12,2]{1,2,0:T(2,128)} %copy-done.47) | copy-start | bytes 580
  197.5 56.8 %copy-start.50 = (f32[2,12,2]{1,2,0:T(2,128)S(1)}, f32[2,12,2]{1,2,0:T(2,128)}, u32[]{:S(2)}) copy-start(f32[2,12,2]{1,2,0:T(2,128)} %copy-done.49) | copy-start | bytes 580
  197.5 56.8 %copy-start.56 = (f32[128]{0:T(128)S(1)}, f32[128]{0:T(128)}, u32[]{:S(2)}) copy-start(f32[128]{0:T(128)} %copy-done.55) | copy-start | bytes 1540
  246.8 9.3 %copy-start.25 = (f32[640,768]{1,0:T(8,128)S(1)}, f32[640,768]{1,0:T(8,128)}, u32[]{:S(2)}) copy-start(f32[640,768]{1,0:T(8,128)} %get-tuple-element.142) | copy-start | bytes 5898244
  256.1 2.0 copy-start.7
  258.1 364.3 %copy-start.1 = (bf16[768,768]{1,0:T(8,128)(2,1)S(1)}, bf16[768,768]{1,0:T(8,128)(2,1)}, u32[]{:S(2)}) copy-start(bf16[768,768]{1,0:T(8,128)(2,1)} %param.34) | copy-start | bytes 3538948
  (12 other events, 8.6 us)
Sparse Core Ops, SparseCore 0:
  11.4 12.6 reduce-scatter.6
  112.1 101.7 reduce-scatter.10
  221.0 118.1 reduce-scatter.8
  345.5 134.8 reduce-scatter.14
  487.8 134.5 reduce-scatter.12
where the time goes:
time: 633 us; the launch traced here: 629 us
  waiting for transfers between devices  354 us (56%)
  matrix products  123 us (19%)
  local copies, waits for them, and re-layouts  56.7 us (9%)
  blocking collectives  47.3 us (7%)
  other arithmetic  32.5 us (5%)
  between operations  15.5 us (2%)
    reduce_scatter x1, waiting for transfers between devices, on_device(): lax.psum_scatter(grad_w_up, ('dp', 'basis'), scatter_dimension=0, tiled=T...  142 us
    reduce_scatter x1, waiting for transfers between devices, on_device(): lax.psum_scatter(grad_w_down, ('dp', 'basis'), scatter_dimension=0, tiled...  141 us
    reduce_scatter x1, waiting for transfers between devices, on_device(): lax.psum_scatter(grad_w_qkv, ('dp', 'basis'), scatter_dimension=0, tiled=...  70.5 us
    unnamed x1, blocking collectives  42.3 us
    unnamed x141, local copies, waits for them, and re-layouts  13.7 us
    dot_general x2, matrix products, on_device(): jnp.einsum('qhe,khe->hqk', upstream, value[:finish], preferred_element_ty...  12.7 us
  transfers between devices with their start and end apart: 5, of which 3 were waited for; matrix products, arithmetic and copies ran while one was open for 23% of the time, Pallas kernels for 0%

commit v1 on v0

--- a/solution.py
+++ b/solution.py
@@ -1,11 +1,19 @@
+import functools
 import math
 
 import jax
 import jax.numpy as jnp
 from jax import lax
+from jax.experimental import pallas as pl
+from jax.experimental.pallas import tpu as pltpu
 from jax.sharding import PartitionSpec as P
 
 eps = 1e-05
+f32 = jnp.float32
+bf16 = jnp.bfloat16
+MESH = pl.DeviceIdType.MESH
+CUT = 32
+STAGES = 5
 
 
 def norm_parts(values, gain, shift):
@@ -40,7 +48,202 @@
     return jnp.where(col_ids <= row_ids, scores, -1e30)
 
 
+class Place:
+    def __init__(self, mesh_shape):
+        self.dp, self.basis = mesh_shape["dp"], mesh_shape["basis"]
+        self.bits = (self.dp * self.basis).bit_length() - 1
+        self.low = self.bits - STAGES
+        self.basis_bits = self.basis.bit_length() - 1
+
+    def here(self):
+        self.me_dp, self.me_basis = lax.axis_index("dp"), lax.axis_index("basis")
+        flat = self.me_dp * self.basis + self.me_basis
+        self.mine = [lax.rem(flat // (1 << (self.low + b)), 2) for b in range(STAGES)]
+
+    def partner(self, b):
+        flip = 1 - 2 * self.mine[b]
+        bit = self.low + b
+        if bit < self.basis_bits:
+            return (self.me_dp, self.me_basis + flip * (1 << bit))
+        return (self.me_dp + flip * (1 << (bit - self.basis_bits)), self.me_basis)
+
+    def spot(self, block, order):
+        where = 0
+        for stage, b in enumerate(order):
+            bit = (block >> b) & 1
+            differs = 1 - self.mine[b] if bit else self.mine[b]
+            where = where + differs * (1 << (STAGES - 1 - stage))
+        return where
+
+
+class Share:
+    def __init__(self, place, order, own, recv, send_sem, recv_sem):
+        self.place, self.order, self.own, self.recv = place, order, own, recv
+        self.send_sem, self.recv_sem = send_sem, recv_sem
+        self.flying = {}
+
+    def send(self, stage):
+        count = CUT >> (stage + 1)
+        copy = pltpu.make_async_remote_copy(
+            src_ref=self.own.at[pl.ds(count, count)],
+            dst_ref=self.recv.at[pl.ds(CUT - 2 * count, count)],
+            send_sem=self.send_sem.at[stage],
+            recv_sem=self.recv_sem.at[stage],
+            device_id=self.place.partner(self.order[stage]),
+            device_id_type=MESH,
+        )
+        copy.start()
+        self.flying[stage] = copy
+
+    def take(self, stage):
+        count = CUT >> (stage + 1)
+        self.flying[stage].wait()
+        if stage == STAGES - 1:
+            return
+        first = CUT - 2 * count
+
+        def add(k, carry):
+            self.own[k] = self.own[k] + self.recv[first + k]
+            return carry
+
+        lax.fori_loop(0, count, add, 0)
+
+    def last(self):
+        return self.own[0].astype(f32) + self.recv[CUT - 2].astype(f32)
+
+
+class Whole:
+    def __init__(self, place, own, recv, send_sem, recv_sem):
+        self.place, self.own, self.recv = place, own, recv
+        self.send_sem, self.recv_sem = send_sem, recv_sem
+        self.flying = {}
+
+    def send(self, stage):
+        copy = pltpu.make_async_remote_copy(
+            src_ref=self.own.at[stage],
+            dst_ref=self.recv.at[stage],
+            send_sem=self.send_sem.at[stage],
+            recv_sem=self.recv_sem.at[stage],
+            device_id=self.place.partner(stage),
+            device_id_type=MESH,
+        )
+        copy.start()
+        self.flying[stage] = copy
+
+    def take(self, stage):
+        self.flying[stage].wait()
+        self.own[stage + 1] = self.own[stage] + self.recv[stage]
+
+
+def greet(place):
+    barrier = pltpu.get_barrier_semaphore()
+    for b in range(STAGES):
+        pl.semaphore_signal(barrier, inc=1, device_id=place.partner(b), device_id_type=MESH)
+    pl.semaphore_wait(barrier, STAGES)
+
+
+ORDERS = ((1, 0, 2, 3, 4), (1, 2, 3, 0, 4), (1, 3, 0, 2, 4))
+
+
+def sum_kernel(place, count, *refs):
+    given, small_in = refs[:count], refs[count]
+    outs, small_out = refs[count + 1 : 2 * count + 1], refs[2 * count + 1]
+    rest = list(refs[2 * count + 2 :])
+    owns, recvs = rest[:count], rest[count : 2 * count]
+    small_own, small_recv, load_sem, send_sem, recv_sem = rest[2 * count :]
+    place.here()
+    shares = [
+        Share(place, ORDERS[i % 3], owns[i], recvs[i], send_sem.at[i], recv_sem.at[i])
+        for i in range(count)
+    ]
+    small = Whole(place, small_own, small_recv, send_sem.at[count], recv_sem.at[count])
+    for i, share in enumerate(shares):
+        for block in range(CUT):
+            pltpu.make_async_copy(
+                given[i].at[block], owns[i].at[place.spot(block, share.order)], load_sem.at[i]
+            ).start()
+    small_own[0] = small_in[...]
+    greet(place)
+    for i, share in enumerate(shares):
+        pltpu.make_async_copy(given[i], owns[i], load_sem.at[i]).wait()
+        share.send(0)
+    small.send(0)
+    for stage in range(STAGES):
+        for share in shares:
+            share.take(stage)
+            if stage < STAGES - 1:
+                share.send(stage + 1)
+        small.take(stage)
+        if stage < STAGES - 1:
+            small.send(stage + 1)
+    for out, share in zip(outs, shares):
+        out[...] = share.last()
+    small_out[...] = small_own[STAGES]
+
+
+def summed_shares(place, arrays, small):
+    count = len(arrays)
+    block = [(a.shape[1], a.shape[2]) for a in arrays]
+    vm = pl.BlockSpec(memory_space=pltpu.VMEM)
+    return pl.pallas_call(
+        lambda *refs: sum_kernel(place, count, *refs),
+        out_shape=[jax.ShapeDtypeStruct(b, f32) for b in block]
+        + [jax.ShapeDtypeStruct(small.shape, f32)],
+        in_specs=[pl.BlockSpec(memory_space=pl.ANY)] * count + [vm],
+        out_specs=[vm] * (count + 1),
+        scratch_shapes=[pltpu.VMEM((CUT,) + b, bf16) for b in block]
+        + [pltpu.VMEM((CUT - 1,) + b, bf16) for b in block]
+        + [
+            pltpu.VMEM((STAGES + 1,) + small.shape, f32),
+            pltpu.VMEM((STAGES,) + small.shape, f32),
+            pltpu.SemaphoreType.DMA((count,)),
+            pltpu.SemaphoreType.DMA((count + 1, STAGES)),
+            pltpu.SemaphoreType.DMA((count + 1, STAGES)),
+        ],
+        compiler_params=pltpu.CompilerParams(
+            collective_id=0, has_side_effects=True, vmem_limit_bytes=56 * 2**20
+        ),
+    )(*arrays, small)
+
+
+def halve_rest(place, rows):
+    for bit in reversed(range(place.low)):
+        half = rows.shape[0] // 2
+        if bit < place.basis_bits:
+            axis, size, mask = "basis", place.basis, 1 << bit
+        else:
+            axis, size, mask = "dp", place.dp, 1 << (bit - place.basis_bits)
+        mine = (lax.axis_index(axis) // mask) % 2
+        keep = lax.dynamic_slice_in_dim(rows, mine * half, half, 0)
+        give = lax.dynamic_slice_in_dim(rows, (1 - mine) * half, half, 0)
+        rows = keep + lax.ppermute(give, axis, [(i, i ^ mask) for i in range(size)])
+    return rows
+
+
+def sum_rest(place, values):
+    for bit in range(place.low):
+        if bit < place.basis_bits:
+            axis, size, mask = "basis", place.basis, 1 << bit
+        else:
+            axis, size, mask = "dp", place.dp, 1 << (bit - place.basis_bits)
+        values = values + lax.ppermute(values, axis, [(i, i ^ mask) for i in range(size)])
+    return values
+
+
+def fold(grad, pieces):
+    rows, columns = grad.shape
+    split = grad.reshape(CUT, rows // CUT, pieces, columns // pieces)
+    return jnp.transpose(split, (0, 2, 1, 3)).reshape(CUT, pieces * rows // CUT, columns // pieces)
+
+
+def unfold(block, pieces):
+    rows, columns = block.shape
+    split = block.reshape(pieces, rows // pieces, columns)
+    return jnp.transpose(split, (1, 0, 2)).reshape(rows // pieces, pieces * columns)
+
+
 def on_device(
+    place,
     tokens,
     w_qkv,
     w_out,
@@ -199,15 +402,24 @@
         grad_hidden_one, normed_one, inverse_one, gain_one
     )
     grad_tokens = (grad_after + grad_resid_norm)[None]
+    grads_of = ((grad_w_down, 1), (grad_w_up, 2), (grad_w_out, 2), (grad_w_qkv, 2))
     small = jnp.stack([grad_gain_one, grad_shift_one, grad_gain_two, grad_shift_two])
-    parts = (
-        lax.psum_scatter(grad_w_qkv, ("dp", "basis"), scatter_dimension=0, tiled=True),
-        lax.psum_scatter(grad_w_out, ("dp", "basis"), scatter_dimension=0, tiled=True),
-        lax.psum_scatter(grad_w_up, ("dp", "basis"), scatter_dimension=0, tiled=True),
-        lax.psum_scatter(grad_w_down, ("dp", "basis"), scatter_dimension=0, tiled=True),
-        lax.psum_scatter(small, ("dp", "basis"), scatter_dimension=1, tiled=True),
-    )
-    share_qkv, share_out, share_up, share_down, share_small = parts
+    small = jnp.concatenate([small, jnp.zeros_like(small)], axis=0)
+    folded = [fold(grad.astype(bf16), pieces) for grad, pieces in grads_of]
+    arrays, widths_of = [], []
+    for array in folded:
+        third = array.shape[2] // 3
+        arrays += [array[:, :, i * third : (i + 1) * third] for i in range(3)]
+    *blocks_of, small = summed_shares(place, arrays, small)
+    shares = []
+    for i, (grad, pieces) in enumerate(grads_of):
+        block = jnp.concatenate(blocks_of[3 * i : 3 * i + 3], axis=1)
+        shares.append(halve_rest(place, unfold(block, pieces)))
+    share_down, share_up, share_out, share_qkv = shares
+    small = sum_rest(place, small)
+    flat = lax.axis_index("dp") * place.basis + lax.axis_index("basis")
+    part = width // (place.dp * place.basis)
+    share_small = lax.dynamic_slice_in_dim(small, flat * part, part, 1)
     return (
         mixed,
         grad_tokens,
@@ -254,5 +466,5 @@
         P(("dp", "basis")),
     )
     return jax.shard_map(
-        on_device, mesh=mesh, in_specs=in_specs, out_specs=out_specs, check_vma=False
-    )
+        functools.partial(on_device, Place(mesh.shape)), mesh=mesh, in_specs=in_specs, out_specs=out_specs, check_vma=False
+    )

time: 633 us -> 337 us (0.53)
  waiting for transfers between devices: 354 us -> 0.02 us
  Pallas kernels: 0 us -> 76.4 us
  blocking collectives: 47.3 us -> 5.51 us
  local copies, waits for them, and re-layouts: 56.7 us -> 82.5 us
  matrix products: 123 us -> 107 us
  other arithmetic: 32.5 us -> 45.3 us
    reduce_scatter x4 -> x0, waiting for transfers between devices: 354 us -> none  [the longest x1 142 us: on_device(): lax.psum_scatter(grad_w_up, ('dp', 'basis'), scatter_dimension=0, tiled=T...]
    pallas_call x0 -> x1, Pallas kernels: none -> 76.4 us  [summed_shares(): pl.pallas_call(lambda *refs: sum_kernel(place, count, *refs), out_shape=[...]
    unnamed x1 -> x0, blocking collectives: 42.3 us -> none
    reshape x0 -> x9, local copies, waits for them, and re-layouts: none -> 27.8 us  [the longest x6 25.7 us: fold(): split = grad.reshape(CUT, rows // CUT, pieces, columns // pieces)]
    slice x0 -> x4, local copies, waits for them, and re-layouts: none -> 7.54 us  [on_device(): arrays += [array[:, :, i * third:(i + 1) * third] for i in range(3)]]
    unnamed x141 -> x122, local copies, waits for them, and re-layouts: 13.7 us -> 7.65 us
  transfers between devices with their start and end apart: 5 -> 1, of which waited for: 3 -> 0; matrix products, arithmetic and copies ran while one was open for 23% -> 13% of each run, Pallas kernels for 0% -> 0%
where the time goes in v1:
time: 337 us; the launch traced here: 332 us
  matrix products  107 us (32%)
  local copies, waits for them, and re-layouts  82.5 us (24%)
  Pallas kernels  76.4 us (23%)
  other arithmetic  45.3 us (13%)
  between operations  15.8 us (5%)
  blocking collectives  5.51 us (2%)
    pallas_call x1, Pallas kernels, summed_shares(): pl.pallas_call(lambda *refs: sum_kernel(place, count, *refs), out_shape=[...  76.4 us
    reshape x6, local copies, waits for them, and re-layouts, fold(): split = grad.reshape(CUT, rows // CUT, pieces, columns // pieces)  25.7 us
    dot_general x2, matrix products, on_device(): jnp.einsum('qhe,khe->hqk', upstream, value[:finish], preferred_element_ty...  13.4 us
    convert_element_type x2, other arithmetic, on_device(): grad_scores = grad_scores.astype(jnp.bfloat16)  11.2 us
    dot_general x2, matrix products, on_device(): jnp.einsum('hqk,khe->qhe', probs, value[:finish], preferred_element_type=...  8.86 us
    dot_general x2, matrix products, on_device(): jnp.einsum('hqk,qhe->khe', probs, upstream, preferred_element_type=jnp.fl...  8.6 us
    unnamed x122, local copies, waits for them, and re-layouts  7.65 us
    slice x4, local copies, waits for them, and re-layouts, on_device(): arrays += [array[:, :, i * third:(i + 1) * third] for i in range(3)]  7.54 us
  transfers between devices with their start and end apart: 1, of which 0 were waited for; matrix products, arithmetic and copies ran while one was open for 13% of the time, Pallas kernels for 0%

profile of v1, /device:TPU:0, one launch (start us, length us, event | category | flops | bytes accessed | tf_op | source)
XLA Modules:
  0.0 332.4 jit_solution(8384251358876908234)
XLA Ops:
  9.3 1.9 convolution_convert_fusion.5
  11.4 1.5 convert_reduce_fusion
  12.9 1.8 fusion.37
  15.4 4.2 %convolution_convert_fusion.2 = bf16[640,2304]{1,0:T(8,128)(2,1)} fusion(bf16[768,2304]{1,0:T(8,128)(2,1)S(1)} %copy-done.6, bf16[1,640,768]{2,1,0:T(8,128)(2,1)S(1)} %copy-done.8, f32[768]{0:T(1024)S(1)} %copy-done.52, f32[768]{0:T(1024)S(1)} %copy-done.45, f32[640]{0:T(1024)S(1)} %add_rsqrt_fusion.1, f32[640]{0:T(1024)S(1)} %broadcast_multiply_fusion.6), kind=kOutput, calls=%fused_computation.24 | convolution fusion | flops 2269347840 | bytes 7482368 | tf_op jit(solution)/shard_map/dot_general | solution.py:273
  19.7 5.7 %copy.98 = bf16[640,2304]{0,1:T(8,128)(2,1)} copy(bf16[640,2304]{1,0:T(8,128)(2,1)} %convolution_convert_fusion.2) | data formatting | bytes 5898240 | tf_op jit(solution)/shard_map/convert_element_type | solution.py:273
  25.4 2.2 slice.304
  27.6 3.4 %fusion.14 = (f32[12,512]{1,0:T(8,128)S(1)}, f32[12,512,512]{1,2,0:T(8,128)S(1)}) fusion(pred[512,512]{0,1:T(8,128)(4,1)S(1)} %iota_compare_fusion, bf16[640,3,12,64]{0,3,2,1:T(8,128)(2,1)} %bitcast.275), kind=kOutput, calls=%fused_computation.27 | convolution fusion | flops 412084224 | bytes 14442496 | tf_op jit(solution)/shard_map/qhe,khe->hqk/dot_general | solution.py:44
  31.1 2.6 fusion
  33.6 1.5 log_add_fusion
  35.6 5.8 %fusion.12 = f32[12,64,512]{2,1,0:T(8,128)} fusion(f32[12,512]{1,0:T(8,128)S(1)} %fusion, f32[12,512]{1,0:T(8,128)S(1)} %get-tuple-element.171, f32[12,512,512]{1,2,0:T(8,128)S(1)} %get-tuple-element.172, pred[512,512]{0,1:T(8,128)(4,1)} %copy-done.14, bf16[640,3,12,64]{0,3,2,1:T(8,128)(2,1)} %bitcast.276), kind=kOutput, calls=%fused_computation.20 | convolution fusion | flops 418381824 | bytes 15253504 | tf_op jit(solution)/shard_map/hqk,khe->qhe/dot_general | solution.py:296
  42.8 2.5 copy.147
  45.2 3.8 %reshape_squeeze.3 = bf16[2,320,12,64]{1,0,3,2:T(2,128)(2,1)} reshape(bf16[640,1,12,64]{0,3,2,1:T(8,128)(2,1)} %slice.304) | data formatting | bytes 1966080 | tf_op jit(solution)/shard_map/reshape;squeeze | solution.py:305
  49.0 2.1 fusion.134
  51.2 1.1 fusion.15
  53.1 3.1 fusion.48
  56.9 1.8 fusion.77
  60.3 1.9 mul.312
  62.2 3.1 mul.313
  65.3 1.7 fusion.66
  67.1 2.4 fusion.44
  69.6 1.1 fusion.135
  71.1 5.4 %fusion.128 = f32[640,3072]{1,0:T(8,128)S(1)} fusion(bf16[768,3072]{1,0:T(8,128)(2,1)} %param.35, f32[640,768]{1,0:T(8,128)S(1)} %get-tuple-element.174, f32[768]{0:T(1024)S(1)} %copy-done.51, f32[768]{0:T(1024)S(1)} %copy-done.44, f32[640]{0:T(1024)S(1)} %add_rsqrt_fusion, f32[640]{0:T(1024)S(1)} %broadcast_multiply_fusion.5), kind=kOutput, calls=%fused_computation.196 | convolution fusion | flops 3022356480 | bytes 14560256 | tf_op jit(solution)/shard_map/dot_general | solution.py:318
  76.6 5.6 %fusion.55 = bf16[1,640,768]{2,1,0:T(8,128)(2,1)} fusion(f32[640,768]{1,0:T(8,128)S(1)} %get-tuple-element.174, bf16[3072,768]{1,0:T(8,128)(2,1)S(1)} %bitcast.317, f32[640,3072]{1,0:T(8,128)S(1)} %fusion.128), kind=kOutput, calls=%fused_computation.90 | convolution fusion | flops 3038576640 | bytes 15532032 | tf_op jit(solution)/shard_map/dot_general | solution.py:321
  82.2 7.4 %fusion.8 = bf16[640,3072]{1,0:T(8,128)(2,1)S(1)} fusion(f32[640,3072]{1,0:T(8,128)S(1)} %fusion.128, bf16[3072,768]{1,0:T(8,128)(2,1)S(1)} %bitcast.317, bf16[1,640,768]{2,1,0:T(8,128)(2,1)S(1)} %copy-done.23), kind=kOutput, calls=%fused_computation.16 | convolution fusion | flops 3059220480 | bytes 17498112 | tf_op jit(solution)/shard_map/dot_general | solution.py:326
  89.6 6.9 %convolution_convert_fusion.1 = bf16[3072,768]{1,0:T(8,128)(2,1)} fusion(bf16[1,640,768]{2,1,0:T(8,128)(2,1)S(1)} %copy-done.23, f32[640,3072]{1,0:T(8,128)S(1)} %fusion.128), kind=kOutput, calls=%fused_computation.23 | convolution fusion | flops 3039952896 | bytes 13565952 | tf_op jit(solution)/shard_map/dot_general | solution.py:325
  96.5 4.2 %multiply_reduce_fusion.2 = (f32[768]{0:T(1024)}, f32[640]{0:T(1024)S(1)}, f32[640]{0:T(1024)S(1)}, f32[768]{0:T(1024)}, f32[640,768]{1,0:T(8,128)S(1)}) fusion(f32[640,768]{1,0:T(8,128)S(1)} %get-tuple-element.174, f32[640]{0:T(1024)S(1)} %add_rsqrt_fusion, f32[640]{0:T(1024)S(1)} %broadcast_multiply_fusion.5, f32[768]{0:T(1024)S(1)} %copy-done.44, ...), kind=kOutput, calls=%fused_computation.73 | convolution fusion | flops 3024319744 | bytes 12602368 | tf_op jit(solution)/shard_map/dot_general | solution.py:329
  100.7 6.2 %convolution_convert_fusion = bf16[768,3072]{1,0:T(8,128)(2,1)} fusion(bf16[640,3072]{1,0:T(8,128)(2,1)S(1)} %fusion.8, f32[640,768]{1,0:T(8,128)S(1)} %get-tuple-element.174, f32[768]{0:T(1024)S(1)} %copy-done.51, f32[768]{0:T(1024)S(1)} %copy-done.44, f32[640]{0:T(1024)S(1)} %add_rsqrt_fusion, f32[640]{0:T(1024)S(1)} %broadcast_multiply_fusion.5), kind=kOutput, calls=%fused_computation.22 | convolution fusion | flops 3024715776 | bytes 10628096 | tf_op jit(solution)/shard_map/dot_general | solution.py:328
  107.7 2.1 convolution_convert_fusion.3
  109.8 1.0 convolution_convert_fusion.4
  110.8 1.3 copy.104
  112.1 3.1 reshape_reshape.3
  116.9 1.1 fusion.71
  118.0 3.1 convolution_bitcast_fusion
  121.4 7.6 %fusion.52 = f32[512,12,64]{0,2,1:T(8,128)} fusion(bf16[512,12,64]{0,2,1:T(8,128)(2,1)S(1)} %bitcast.293, f32[12,512]{1,0:T(8,128)S(1)} %copy-done.24, f32[12,512,512]{1,2,0:T(8,128)} %copy-done.2, pred[512,512]{0,1:T(8,128)(4,1)S(1)} %copy-done.15), kind=kOutput, calls=%fused_computation.88 | convolution fusion | flops 415236096 | bytes 15228928 | tf_op jit(solution)/shard_map/hqk,qhe->khe/dot_general | solution.py:379
  129.0 9.6 %multiply_reduce_fusion = (f32[12,512]{1,0:T(8,128)S(1)}, f32[12,512,512]{1,2,0:T(8,128)}) fusion(f32[12,512]{1,0:T(8,128)S(1)} %copy-done.24, f32[12,512,512]{1,2,0:T(8,128)} %copy-done.2, pred[512,512]{0,1:T(8,128)(4,1)S(1)} %copy-done.15, bf16[512,12,64]{0,2,1:T(8,128)(2,1)S(1)} %bitcast.294, bf16[640,3,12,64]{0,3,2,1:T(8,128)(2,1)} %bitcast.279), kind=kOutput, calls=%fused_computation.1 | convolution fusion | flops 418375680 | bytes 27049984 | tf_op jit(solution)/shard_map/qhe,khe->hqk/dot_general | solution.py:371
  138.8 1.0 mul.348
  139.8 2.6 mul.349
  142.6 3.8 %multiply_reduce_fusion.1 = (f32[12,128]{1,0:T(8,128)S(1)}, f32[12,128,640]{2,1,0:T(8,128)S(1)}) fusion(f32[12,128,640]{2,1,0:T(8,128)} %copy-done.3, f32[12,128]{1,0:T(8,128)S(1)} %log_add_fusion.1, bf16[128,12,64]{0,2,1:T(8,128)(2,1)S(1)} %bitcast.299, bf16[640,3,12,64]{0,3,2,1:T(8,128)(2,1)} %bitcast.280), kind=kOutput, calls=%fused_computation.29 | convolution fusion | flops 128776704 | bytes 9056256 | tf_op jit(solution)/shard_map/qhe,khe->hqk/dot_general | solution.py:371
  146.7 1.0 fusion.45
  147.7 9.9 %multiply_convert_fusion = bf16[12,512,512]{1,2,0:T(8,128)(2,1)S(1)} fusion(f32[12,512,512]{1,2,0:T(8,128)} %get-tuple-element.177, f32[12,512]{1,0:T(8,128)S(1)} %get-tuple-element.176, f32[12,512]{1,0:T(8,128)S(1)} %copy-done.24, f32[12,512,512]{1,2,0:T(8,128)} %copy-done.2, pred[512,512]{0,1:T(8,128)(4,1)S(1)} %copy-done.15), kind=kLoop, calls=%fused_computation | loop fusion | flops 18874368 | bytes 31768576 | tf_op jit(solution)/shard_map/convert_element_type | solution.py:377
  157.6 2.0 multiply_bitcast_fusion
  159.8 1.1 fusion.51
  161.1 1.3 multiply_convert_fusion.2
  164.3 1.5 copy-done.7
  166.1 4.2 %fusion.36 = (f32[768]{0:T(1024)S(1)}, f32[640]{0:T(1024)S(1)}, f32[640]{0:T(1024)S(1)}, f32[768]{0:T(1024)S(1)}, f32[640,768]{1,0:T(8,128)}) fusion(bf16[1,640,768]{2,1,0:T(8,128)(2,1)S(1)} %copy-done.10, f32[640]{0:T(1024)S(1)} %copy-done.37, f32[640]{0:T(1024)S(1)} %copy-done.32, f32[768]{0:T(1024)S(1)} %copy-done.46, ...), kind=kOutput, calls=%fused_computation.59 | convolution fusion | flops 2269836544 | bytes 9456640 | tf_op jit(solution)/shard_map/dot_general | solution.py:400
  170.3 5.6 %fusion.81 = f32[768,2304]{1,0:T(8,128)} fusion(bf16[640,2304]{0,1:T(8,128)(2,1)S(1)} %bitcast.296, bf16[1,640,768]{2,1,0:T(8,128)(2,1)S(1)} %copy-done.10, f32[768]{0:T(1024)S(1)} %copy-done.53, f32[768]{0:T(1024)S(1)} %copy-done.46, f32[640]{0:T(1024)S(1)} %copy-done.37, f32[640]{0:T(1024)S(1)} %copy-done.32), kind=kOutput, calls=%fused_computation.112 | convolution fusion | flops 2267873280 | bytes 11021312 | tf_op jit(solution)/shard_map/dot_general | solution.py:398
  175.9 2.3 fusion.131
  178.3 11.6 %reshape.420 = bf16[32,24,2,1536]{3,2,1,0:T(2,128)(2,1)} reshape(bf16[768,3072]{1,0:T(8,128)(2,1)} %convolution_convert_fusion) | data formatting | bytes 9437184 | tf_op jit(solution)/shard_map/reshape | solution.py:235
  189.9 3.3 %copy.113 = bf16[32,24,2,1536]{3,1,2,0:T(8,128)(2,1)S(1)} copy(bf16[32,24,2,1536]{3,2,1,0:T(2,128)(2,1)} %reshape.420) | data formatting | bytes 9437184 | tf_op jit(solution)/shard_map/reshape | solution.py:235
  193.2 2.2 fusion.130
  196.0 1.1 fusion.133
  197.1 5.5 %all-gather = bf16[24,2,768]{2,1,0:T(2,128)(2,1)S(1)} all-gather(bf16[12,2,768]{2,1,0:T(2,128)(2,1)S(1)} %copy-done.33), channel_id=2, replica_groups=mesh['dp'=16,'basis'=2] {'basis'}, dimensions={0}, use_global_device_ids=true | all-gather | bytes 110592 | tf_op jit(solution)/shard_map/all_gather | solution.py:358
  202.6 1.3 convolution_bitcast_fusion.1
  203.9 4.9 %copy.116 = f32[768,2,12,64]{0,3,2,1:T(8,128)} copy(f32[768,2,12,64]{0,3,1,2:T(8,128)} %convolution_bitcast_fusion) | data formatting | bytes 9437184 | tf_op jit(solution)/shard_map/hbd,chbe->dche/transpose | solution.py:352
  208.8 6.2 %copy.117 = f32[768,1536]{1,0:T(8,128)} copy(f32[768,1536]{0,1:T(8,128)} %bitcast.286) | data formatting | bytes 9437184 | tf_op jit(solution)/shard_map/reshape.207
  215.0 6.9 %fusion.13 = f32[768,2304]{1,0:T(8,128)} fusion(f32[768,2304]{1,0:T(8,128)} %fusion.81, f32[768,1536]{1,0:T(8,128)} %copy.117), kind=kLoop, calls=%fused_computation.26 | loop fusion | flops 1179648 | bytes 14155776 | tf_op jit(solution)/shard_map/scatter-add | solution.py:399
  221.9 5.2 %convert_element_type.182 = bf16[768,2304]{1,0:T(8,128)(2,1)} convert(f32[768,2304]{1,0:T(8,128)} %fusion.13) | non-fusion elementwise | flops 1769472 | bytes 10616832 | tf_op jit(solution)/shard_map/convert_element_type | solution.py:408
  227.1 7.9 %reshape.425 = bf16[32,24,2,1152]{3,2,1,0:T(2,128)(2,1)} reshape(bf16[768,2304]{1,0:T(8,128)(2,1)} %convert_element_type.182) | data formatting | bytes 7077888 | tf_op jit(solution)/shard_map/reshape | solution.py:235
  235.0 2.5 copy.118
  237.4 1.9 fusion.132
  240.0 76.4 %shard_map.231 = (f32[96,256]{1,0:T(8,128)}, f32[96,256]{1,0:T(8,128)}, f32[96,256]{1,0:T(8,128)}, f32[48,512]{1,0:T(8,128)}, f32[48,512]{1,0:T(8,128)}, /*index...) custom-call(bf16[32,96,256]{2,1,0:T(8,128)(2,1)} %get-tuple-element., ...), custom_call_target="tpu_custom_call" | custom-call | tf_op jit(solution)/shard_map/pallas_call | solution.py:188
  316.4 1.1 pad_maximum_fusion.2
  320.9 1.0 pad_maximum_fusion
  322.7 1.9 fusion.35
  (182 shorter events, 19.7 us)
Async XLA Ops:
  7.2 62.4 %copy-start = (bf16[768,768]{1,0:T(8,128)(2,1)S(1)}, bf16[768,768]{1,0:T(8,128)(2,1)}, u32[]{:S(2)}) copy-start(bf16[768,768]{1,0:T(8,128)(2,1)} %param.34) | copy-start | bytes 3538948
  7.2 49.7 %reduce-scatter.2.cloned.1.call-start = ((), (), s32[]{:S(2)}) async-start(), calls=%async_computation.1 | async-start | bytes 147456 | tf_op jit(solution)/shard_map/reduce_scatter | solution.py:281
  7.3 1.5 copy-start.49
  8.0 0.7 copy-start.42
  8.7 0.6 copy-start.38
  8.7 0.6 copy-start.40
  11.3 19.7 %copy-start.14 = (pred[512,512]{0,1:T(8,128)(4,1)}, pred[512,512]{0,1:T(8,128)(4,1)S(1)}, u32[]{:S(2)}) copy-start(pred[512,512]{0,1:T(8,128)(4,1)S(1)} %iota_compare_fusion) | copy-start | bytes 786436
  12.9 2.4 copy-start.6
  12.9 2.6 copy-start.8
  12.9 2.5 copy-start.45
  12.9 2.5 copy-start.52
  12.9 1.8 copy-start.31
  14.7 0.6 copy-start.36
  31.1 4.5 %copy-start.2 = (f32[12,512,512]{1,2,0:T(8,128)}, f32[12,512,512]{1,2,0:T(8,128)S(1)}, u32[]{:S(2)}) copy-start(f32[12,512,512]{1,2,0:T(8,128)S(1)} %get-tuple-element.172) | copy-start | bytes 37748740
  35.6 7.2 %slice-start = ((bf16[768,2304]{1,0:T(8,128)(2,1)}), bf16[768,1536]{1,0:T(8,128)(2,1)S(1)}, s32[]{:S(2)}) async-start(bf16[768,2304]{1,0:T(8,128)(2,1)} %param.33), calls=%async_computation.2 | async-start | bytes 4718592 | tf_op jit(solution)/shard_map/slice | solution.py:299
  51.2 1.9 copy-start.3
  53.1 3.1 copy-start.34
  53.1 3.8 %copy-start.18 = (bf16[768,1536]{0,1:T(8,128)(2,1)S(1)}, bf16[768,1536]{0,1:T(8,128)(2,1)}, u32[]{:S(2)}) copy-start(bf16[768,1536]{0,1:T(8,128)(2,1)} %copy.147) | copy-start | bytes 7077892
  65.3 4.3 %copy-start.9 = (bf16[1,640,768]{2,1,0:T(8,128)(2,1)S(1)}, bf16[1,640,768]{2,1,0:T(8,128)(2,1)}, u32[]{:S(2)}) copy-start(bf16[1,640,768]{2,1,0:T(8,128)(2,1)} %param.32) | copy-start | bytes 2949124
  69.6 1.5 copy-start.44
  69.6 1.5 copy-start.51
  69.6 6.9 %slice-start.5 = ((s8[4718592]{0:T(1024)(128)(4,1)}), s8[4194304]{0:T(1024)(128)(4,1)S(1)}, s32[]{:S(2)}) async-start(s8[4718592]{0:T(1024)(128)(4,1)} %bitcast.316), calls=%async_computation.7 | async-start | bytes 8388608
  71.1 5.4 %slice-start.6 = ((s8[4718592]{0:T(1024)(128)(4,1)}), s8[524288]{0:T(1024)(128)(4,1)S(1)}, s32[]{:S(2)}) async-start(s8[4718592]{0:T(1024)(128)(4,1)} %bitcast.316), calls=%async_computation.8 | async-start | bytes 1048576
  76.6 5.6 %copy-start.23 = (bf16[1,640,768]{2,1,0:T(8,128)(2,1)S(1)}, bf16[1,640,768]{2,1,0:T(8,128)(2,1)}, u32[]{:S(2)}) copy-start(bf16[1,640,768]{2,1,0:T(8,128)(2,1)} %param.45) | copy-start | bytes 2949124
  76.6 19.9 %slice-start.7 = ((s8[4718592]{0:T(1024)(128)(4,1)}), s8[4194304]{0:T(1024)(128)(4,1)S(1)}, s32[]{:S(2)}) async-start(s8[4718592]{0:T(1024)(128)(4,1)} %bitcast.318), calls=%async_computation.9 | async-start | bytes 8388608
  82.2 14.3 %slice-start.8 = ((s8[4718592]{0:T(1024)(128)(4,1)}), s8[524288]{0:T(1024)(128)(4,1)S(1)}, s32[]{:S(2)}) async-start(s8[4718592]{0:T(1024)(128)(4,1)} %bitcast.318), calls=%async_computation.10 | async-start | bytes 1048576
  107.6 3.1 copy-start.11
  110.8 4.5 %copy-start.17 = (bf16[640,768]{1,0:T(8,128)(2,1)}, bf16[640,768]{1,0:T(8,128)(2,1)S(1)}, u32[]{:S(2)}) copy-start(bf16[640,768]{1,0:T(8,128)(2,1)S(1)} %convolution_convert_fusion.4) | copy-start | bytes 2949124
  110.8 5.4 %copy-start.16 = (bf16[2,320,12,64]{1,0,3,2:T(2,128)(2,1)S(1)}, bf16[2,320,12,64]{1,0,3,2:T(2,128)(2,1)}, u32[]{:S(2)}) copy-start(bf16[2,320,12,64]{1,0,3,2:T(2,128)(2,1)} %reshape_squeeze.3) | copy-start | bytes 2949124
  115.2 1.7 copy-start.19
  115.2 2.8 copy-start.35
  116.1 4.9 %copy-start.25 = (f32[2,12,320]{2,0,1:T(2,128)}, f32[2,12,320]{2,0,1:T(2,128)S(1)}, u32[]{:S(2)}) copy-start(f32[2,12,320]{2,0,1:T(2,128)S(1)} %fusion.106) | copy-start | bytes 92164
  118.0 3.1 slice-start.4
  118.0 3.4 %copy-start.15 = (pred[512,512]{0,1:T(8,128)(4,1)S(1)}, pred[512,512]{0,1:T(8,128)(4,1)}, u32[]{:S(2)}) copy-start(pred[512,512]{0,1:T(8,128)(4,1)} %copy-done.14) | copy-start | bytes 786436
  118.0 3.4 %copy-start.24 = (f32[12,512]{1,0:T(8,128)S(1)}, f32[12,512]{1,0:T(8,128)}, u32[]{:S(2)}) copy-start(f32[12,512]{1,0:T(8,128)} %log_add_fusion) | copy-start | bytes 73732
  129.0 9.6 %copy-start.30 = (f32[2,12,64]{2,0,1:T(2,128)S(1)}, f32[2,12,64]{2,0,1:T(2,128)}, u32[]{:S(2)}) copy-start(f32[2,12,64]{2,0,1:T(2,128)} %get-tuple-element.162) | copy-start | bytes 18436
  138.8 3.6 %slice-start.3 = ((bf16[640,768]{1,0:T(8,128)(2,1)}), bf16[128,768]{1,0:T(8,128)(2,1)S(1)}, s32[]{:S(2)}) async-start(bf16[640,768]{1,0:T(8,128)(2,1)} %copy-done.17), calls=%async_computation.5 | async-start | bytes 393216 | tf_op jit(solution)/shard_map/slice | solution.py:370
  139.8 2.7 copy-start.26
  142.6 3.8 %copy-start.4 = (f32[12,128,640]{2,1,0:T(8,128)S(1)}, f32[12,128,640]{2,1,0:T(8,128)}, u32[]{:S(2)}) copy-start(f32[12,128,640]{2,1,0:T(8,128)} %copy-done.3) | copy-start | bytes 11796484
  142.6 4.1 %copy-start.21 = (f32[512,12,64]{0,2,1:T(8,128)S(1)}, f32[512,12,64]{0,2,1:T(8,128)}, u32[]{:S(2)}) copy-start(f32[512,12,64]{0,2,1:T(8,128)} %fusion.52) | copy-start | bytes 4718596
  147.7 9.9 %copy-start.5 = (bf16[640,2304]{0,1:T(8,128)(2,1)S(1)}, bf16[640,2304]{0,1:T(8,128)(2,1)}, u32[]{:S(2)}) copy-start(bf16[640,2304]{0,1:T(8,128)(2,1)} %copy.98) | copy-start | bytes 8847364
  157.6 2.0 copy-start.13
  162.4 1.9 copy-start.32
  162.4 1.9 copy-start.37
  162.5 1.9 copy-start.46
  163.9 2.0 copy-start.7
  163.9 2.3 copy-start.10
  163.9 12.0 %slice-start.1 = ((s8[4718592]{0:T(1024)(128)(4,1)}), s8[4194304]{0:T(1024)(128)(4,1)S(1)}, s32[]{:S(2)}) async-start(s8[4718592]{0:T(1024)(128)(4,1)} %bitcast.289), calls=%async_computation.3 | async-start | bytes 8388608
  166.1 4.2 %copy-start.53 = (f32[768]{0:T(1024)S(1)}, f32[768]{0:T(1024)}, u32[]{:S(2)}) copy-start(f32[768]{0:T(1024)} %param.38) | copy-start | bytes 9220
  166.1 9.8 %slice-start.2 = ((s8[4718592]{0:T(1024)(128)(4,1)}), s8[524288]{0:T(1024)(128)(4,1)S(1)}, s32[]{:S(2)}) async-start(s8[4718592]{0:T(1024)(128)(4,1)} %bitcast.289), calls=%async_computation.4 | async-start | bytes 1048576
  175.9 2.3 copy-start.48
  175.9 2.3 copy-start.47
  193.2 2.2 copy-start.22
  195.8 1.3 copy-start.33
  195.8 6.8 %copy-start.39 = (f32[2,12,2]{1,2,0:T(2,128)S(1)}, f32[2,12,2]{1,2,0:T(2,128)}, u32[]{:S(2)}) copy-start(f32[2,12,2]{1,2,0:T(2,128)} %copy-done.38) | copy-start | bytes 580
  195.8 6.8 %copy-start.41 = (f32[2,12,2]{1,2,0:T(2,128)S(1)}, f32[2,12,2]{1,2,0:T(2,128)}, u32[]{:S(2)}) copy-start(f32[2,12,2]{1,2,0:T(2,128)} %copy-done.40) | copy-start | bytes 580
  195.8 6.8 %copy-start.43 = (f32[2,12,2]{1,2,0:T(2,128)S(1)}, f32[2,12,2]{1,2,0:T(2,128)}, u32[]{:S(2)}) copy-start(f32[2,12,2]{1,2,0:T(2,128)} %copy-done.42) | copy-start | bytes 580
  195.8 6.8 %copy-start.50 = (f32[128]{0:T(128)S(1)}, f32[128]{0:T(128)}, u32[]{:S(2)}) copy-start(f32[128]{0:T(128)} %copy-done.49) | copy-start | bytes 1540
  240.0 82.7 %copy-start.20 = (f32[640,768]{1,0:T(8,128)S(1)}, f32[640,768]{1,0:T(8,128)}, u32[]{:S(2)}) copy-start(f32[640,768]{1,0:T(8,128)} %get-tuple-element.180) | copy-start | bytes 5898244
  316.4 6.3 %copy-start.12 = (f32[640,768]{1,0:T(8,128)S(1)}, f32[640,768]{1,0:T(8,128)}, u32[]{:S(2)}) copy-start(f32[640,768]{1,0:T(8,128)} %copy-done.11) | copy-start | bytes 5898244
  322.7 2.7 copy-start.1
  322.7 2.0 copy-start.27
  322.7 2.0 copy-start.28
  322.7 2.0 copy-start.29
Sparse Core Ops, SparseCore 0:
  11.4 12.6 reduce-scatter.1

commit v2 on v0

v2 whole, which is shorter than its diff:
```python
import functools, math
import jax, jax.numpy as jnp
from jax import lax
from jax.experimental import pallas as pl
from jax.experimental.pallas import tpu as pltpu
from jax.sharding import PartitionSpec as P
f32 = jnp.float32; bf16 = jnp.bfloat16
eps = 1e-05
ANY = pl.BlockSpec(memory_space=pl.ANY)
VM = pl.BlockSpec(memory_space=pltpu.VMEM)
SM = pl.BlockSpec(memory_space=pltpu.SMEM)
LANES=128

def nn(a, b):
    return jnp.dot(a, b, preferred_element_type=f32)
def nt(a, b):
    return lax.dot_general(a, b, (((1,), (1,)), ((), ())), preferred_element_type=f32)
def tn(a, b):
    return lax.dot_general(a, b, (((0,), (0,)), ((), ())), preferred_element_type=f32)

def lanes_of(c):
    return pl.ds(pl.multiple_of(c * LANES, LANES), LANES)
def rows_of(i, n):
    return pl.ds(pl.multiple_of(i * n, n), n)

def query_blocks(seq):
    wide = 256
    return [(q, min(wide, seq - q)) for q in range(0, seq, wide)]

def causal(scores, first):
    keys, queries = scores.shape
    top, low = scores[:first], scores[first:]
    key = lax.broadcasted_iota(jnp.int32, low.shape, 0)
    query = lax.broadcasted_iota(jnp.int32, low.shape, 1)
    low = jnp.where(key <= query, low, -1e30)
    return low if first == 0 else jnp.concatenate([top, low], axis=0)

def norm_into(src, out, gain, shift, seq):
    def body(c, carry):
        at = lanes_of(c)
        x = src[:, at]
        cen = x - jnp.mean(x, axis=0, keepdims=True)
        inv = lax.rsqrt(jnp.mean(cen * cen, axis=0, keepdims=True) + eps)
        out[:, at] = (cen * inv * gain + shift).astype(out.dtype)
        return carry
    lax.fori_loop(0, seq // LANES, body, 0)

def mem_columns(block, head):
    lane = lax.broadcasted_iota(jnp.int32, block.shape, 1)
    wide = block.astype(f32)
    return [jnp.sum(jnp.where(lane == 2 * head + b, wide, 0.0), axis=1, keepdims=True) for b in (0, 1)]

def by_block(columns, shape, span):
    lane = lax.broadcasted_iota(jnp.int32, shape, 1)
    return jnp.where(lane < span, columns[0], columns[1])

def forward_kernel(heads, span, scale,
    flag, tokens_h, norms, memory, w_qkv_h, w_out_h, w_up_h,
    h1_o, qkv_o, aux_o, joined_o, after_o, h2_o, act_o, slope_o,
    tokens, w_qkv, w_out, w_up, x, h1, qkv, aux, joined, after, h2, act, slope, in_sem, out_sem):
    seq, width = tokens.shape
    ff = w_up.shape[1]
    hd = width // heads
    loads = [pltpu.make_async_copy(s, d, in_sem.at[i]) for i, (s, d) in enumerate(
        [(tokens_h, tokens), (w_qkv_h, w_qkv), (w_out_h, w_out), (w_up_h, w_up)])]
    for l in loads: l.start()
    def put(i, src, dst):
        cp = pltpu.make_async_copy(src, dst, out_sem.at[i]); cp.start(); return cp
    puts = []
    gain = norms[:, 0:1]; shift = norms[:, 1:2]
    h1[:, seq:] = jnp.transpose(memory[...].astype(f32)).astype(bf16)
    loads[0].wait()
    def turn(c, carry):
        at = lanes_of(c)
        x[:, at] = jnp.transpose(tokens[at, :].astype(f32))
        return carry
    lax.fori_loop(0, seq // LANES, turn, 0)
    norm_into(x, h1, gain, shift, seq)
    puts.append(put(0, h1, h1_o))
    loads[1].wait()
    def project(i, carry):
        at = rows_of(i, width)
        qkv[at, :] = tn(w_qkv[:, at], h1[...]).astype(bf16)
        return carry
    lax.fori_loop(0, 3, project, 0)
    puts.append(put(1, qkv, qkv_o))
    on = flag[0].astype(f32)
    sub = lax.broadcasted_iota(jnp.int32, (8, seq), 0)

    def head_step(h, carry):
        base = pl.multiple_of(h * hd, hd)
        q = qkv[pl.ds(base, hd), :seq] * jnp.asarray(scale, bf16)
        kx = jnp.transpose(qkv[pl.ds(width + base, hd), :])
        v = qkv[pl.ds(2 * width + base, hd), :seq]
        outs, logs = [], []
        for first, n in query_blocks(seq):
            keys = first + n
            s = causal(nn(kx[:keys], q[:, first:keys]), first)
            peak = jnp.max(s, axis=0, keepdims=True)
            e = jnp.exp(s - peak)
            total = jnp.sum(e, axis=0, keepdims=True)
            outs.append(nn(v[:, :keys], e.astype(bf16)) / total)
            logs.append(peak + jnp.log(total))
        o = jnp.concatenate(outs, axis=1)
        log_total = jnp.concatenate(logs, axis=1)
        ms = nn(kx[seq:seq + 32], q)
        row = lax.broadcasted_iota(jnp.int32, ms.shape, 0)
        lane = lax.broadcasted_iota(jnp.int32, ms.shape, 1)
        want = 2 * h + jnp.where(lane < span, 0, 1)
        ms = jnp.sum(jnp.where(row == want, ms, 0.0), axis=0, keepdims=True)
        sig = jax.nn.sigmoid(ms)
        mv = by_block(mem_columns(qkv[pl.ds(2 * width + base, hd), seq:], h), (hd, seq), span)
        joined[pl.ds(base, hd), :] = (o + (sig * on) * mv).astype(bf16)
        aux[h] = jnp.where(sub == 0, log_total, jnp.where(sub == 1, sig, 0.0))
        return carry
    lax.fori_loop(0, heads, head_step, 0)
    puts.append(put(2, aux, aux_o))
    puts.append(put(3, joined, joined_o))
    loads[2].wait()
    after[...] = x[...] + tn(w_out[...], joined[...])
    puts.append(put(4, after, after_o))
    norm_into(after, h2, norms[:, 2:3], norms[:, 3:4], seq)
    puts.append(put(5, h2, h2_o))
    loads[3].wait()
    step = 512
    def up(i, carry):
        at = rows_of(i, step)
        pre = tn(w_up[:, at], h2[...])
        sq = pre * pre
        c = math.sqrt(2.0 / math.pi)
        t = jnp.tanh(pre * (c + (c * 0.044715) * sq))
        half = 0.5 + 0.5 * t
        act[at, :] = (pre * half).astype(bf16)
        slope[at, :] = (half + (0.5 * pre) * (1.0 - t * t) * (c + (3 * c * 0.044715) * sq)).astype(bf16)
        return carry
    lax.fori_loop(0, ff // step, up, 0)
    puts.append(put(6, act, act_o))
    puts.append(put(7, slope, slope_o))
    for p in puts: p.wait()

def forward(heads, blocks, flag, tokens, norms, memory, w_qkv, w_out, w_up):
    seq, width = tokens.shape
    ff = w_up.shape[1]
    wide = seq + LANES
    span = seq // blocks
    scale = 1.0 / math.sqrt(width // heads)
    S = jax.ShapeDtypeStruct
    outs = [((width, wide), bf16), ((3 * width, wide), bf16), ((heads, 8, seq), f32), ((width, seq), bf16),
            ((width, seq), f32), ((width, seq), bf16), ((ff, seq), bf16), ((ff, seq), bf16)]
    return pl.pallas_call(
        functools.partial(forward_kernel, heads, span, scale),
        out_shape=[S(*o) for o in outs],
        in_specs=[SM, ANY, VM, VM, ANY, ANY, ANY],
        out_specs=[ANY] * len(outs),
        scratch_shapes=[pltpu.VMEM(tokens.shape, bf16), pltpu.VMEM(w_qkv.shape, bf16), pltpu.VMEM(w_out.shape, bf16), pltpu.VMEM(w_up.shape, bf16),
            pltpu.VMEM((width, seq), f32)] + [pltpu.VMEM(*o) for o in outs] + [pltpu.SemaphoreType.DMA((4,)), pltpu.SemaphoreType.DMA((len(outs),))],
        compiler_params=pltpu.CompilerParams(vmem_limit_bytes=56 * 2**20),
    )(flag, tokens, norms, memory, w_qkv, w_out, w_up)

GROUP = 32
STAGES = 5
MESH = pl.DeviceIdType.MESH

class Place:
    def __init__(self, mesh_shape):
        self.dp, self.basis = mesh_shape["dp"], mesh_shape["basis"]
        self.bits = (self.dp * self.basis).bit_length() - 1
        self.low = self.bits - STAGES
        self.basis_bits = self.basis.bit_length() - 1

    def here(self):
        self.me_dp, self.me_basis = lax.axis_index("dp"), lax.axis_index("basis")
        flat = self.me_dp * self.basis + self.me_basis
        self.mine = [lax.rem(flat // (1 << (self.low + b)), 2) for b in range(STAGES)]

    def partner(self, b):
        flip = 1 - 2 * self.mine[b]
        bit = self.low + b
        if bit < self.basis_bits:
            return (self.me_dp, self.me_basis + flip * (1 << bit))
        return (self.me_dp + flip * (1 << (bit - self.basis_bits)), self.me_basis)

    def beside(self):
        return (self.me_dp, 1 - self.me_basis)

    def spot(self, block, order):
        where = 0
        for stage, b in enumerate(order):
            differs = 1 - self.mine[b] if (block >> b) & 1 else self.mine[b]
            where = where + differs * (1 << (STAGES - 1 - stage))
        return where


class Share:
    def __init__(self, place, order, own, recv, send_sem, recv_sem, columns=None):
        self.place, self.order, self.own, self.recv = place, order, own, recv
        self.send_sem, self.recv_sem = send_sem, recv_sem
        self.columns = own.shape[2] if columns is None else columns
        self.sent = None
        self.stage = 0

    def store(self, block, value, first=0):
        self.own[self.place.spot(block, self.order), :, first : first + value.shape[1]] = value.astype(bf16)

    def send(self):
        stage = self.stage
        count = GROUP >> (stage + 1)
        self.sent = pltpu.make_async_remote_copy(
            src_ref=self.own.at[pl.ds(count, count), :, pl.ds(0, self.columns)],
            dst_ref=self.recv.at[pl.ds(GROUP - 2 * count, count), :, pl.ds(0, self.columns)],
            send_sem=self.send_sem.at[stage],
            recv_sem=self.recv_sem.at[stage],
            device_id=self.place.partner(self.order[stage]),
            device_id_type=MESH,
        )
        self.sent.start()

    def pump(self):
        self.sent.wait()
        count = GROUP >> (self.stage + 1)
        self.stage += 1
        if self.stage == STAGES:
            return
        first = GROUP - 2 * count
        at = pl.ds(0, self.columns)

        def add(k, carry):
            self.own[k, :, at] = self.own[k, :, at] + self.recv[first + k, :, at]
            return carry

        lax.fori_loop(0, count, add, 0)
        self.send()

    def last(self):
        at = pl.ds(0, self.columns)
        return self.own[0, :, at].astype(f32) + self.recv[GROUP - 2, :, at].astype(f32)


class Whole:
    def __init__(self, place, own, recv, send_sem, recv_sem):
        self.place, self.own, self.recv = place, own, recv
        self.send_sem, self.recv_sem = send_sem, recv_sem
        self.stage = 0

    def send(self):
        stage = self.stage
        self.sent = pltpu.make_async_remote_copy(
            src_ref=self.own.at[stage], dst_ref=self.recv.at[stage],
            send_sem=self.send_sem.at[stage], recv_sem=self.recv_sem.at[stage],
            device_id=self.place.partner(stage), device_id_type=MESH)
        self.sent.start()

    def pump(self):
        self.sent.wait()
        stage = self.stage
        self.own[stage + 1] = self.own[stage] + self.recv[stage]
        self.stage += 1
        if self.stage < STAGES:
            self.send()


def greet(place):
    barrier = pltpu.get_barrier_semaphore()
    for b in range(STAGES):
        pl.semaphore_signal(barrier, inc=1, device_id=place.partner(b), device_id_type=MESH)
    if place.low > 0:
        pl.semaphore_signal(barrier, inc=1, device_id=place.beside(), device_id_type=MESH)
    pl.semaphore_wait(barrier, STAGES + (1 if place.low > 0 else 0))


ORDERS = ((1, 0, 2, 3, 4), (1, 2, 3, 0, 4), (1, 3, 0, 2, 4))


def norm_back(x_of, u_of, out, gain, acc_gain, acc_shift, chunks, base_of):
    acc_gain[...] = jnp.zeros_like(acc_gain)
    acc_shift[...] = jnp.zeros_like(acc_shift)

    def body(c, carry):
        at = lanes_of(c)
        x = x_of(c)
        cen = x - jnp.mean(x, axis=0, keepdims=True)
        inv = lax.rsqrt(jnp.mean(cen * cen, axis=0, keepdims=True) + eps)
        n = cen * inv
        u = u_of(c)
        un = u * n
        acc_gain[...] += un
        acc_shift[...] += u
        g = u * gain
        m1 = jnp.mean(g, axis=0, keepdims=True)
        m2 = jnp.mean(un * gain, axis=0, keepdims=True)
        out(c, base_of(c) + inv * (g - m1 - n * m2))
        return carry

    lax.fori_loop(0, chunks, body, 0)


def columns_sum(acc):
    return jnp.sum(jnp.transpose(acc[...]), axis=0, keepdims=True)


def backward_kernel(place, heads, span, scale,
    flag, norms, weights_e, dy_h, tokens_h, act_h, slope_h, h2_h, after_h, joined_h, qkv_h, aux_h, h1_h, w_down_h, w_up_h, w_out_h, w_qkv_h,
    mixed_o, gtok_o, gcoef_o, s_qkv, s_out, s_up, s_down, small_o,
    dy, act, slope, h2, joined, qkv, aux, h1, w_down, w_up, x, g, da, acc_a, acc_b, rows_small,
    own_d, own_u, own_o, recv_d, recv_u, recv_o, mem_own, mem_recv,
    small_own, small_recv, load_sem, out_sem, send_sem, recv_sem, ready_sem, mem_sem):
    width, seq = h2.shape
    ff = act.shape[0]
    hd = width // heads
    chunks = seq // LANES
    place.here()
    barrier_parts = None
    loads = {}

    def load(name, src, dst):
        cp = pltpu.make_async_copy(src, dst, load_sem.at[len(loads)])
        cp.start()
        loads[name] = cp

    load("dy", dy_h, dy)
    load("act", act_h, act)
    load("w_down", w_down_h, w_down)
    load("slope", slope_h, slope)
    load("h2", h2_h, h2)
    load("w_up", w_up_h, w_up)
    load("after", after_h, x)
    load("joined", joined_h, joined)
    load("qkv", qkv_h, qkv)
    load("aux", aux_h, aux)
    load("h1", h1_h, h1)
    greet(place)
    down = [Share(place, ORDERS[p], own_d.at[p], recv_d.at[p], send_sem.at[p], recv_sem.at[p]) for p in range(3)]
    up = [Share(place, ORDERS[p], own_u.at[p], recv_u.at[p], send_sem.at[3 + p], recv_sem.at[3 + p]) for p in range(3)]
    out = Share(place, ORDERS[2], own_o, recv_o, send_sem.at[6], recv_sem.at[6])
    small = Whole(place, small_own, small_recv, send_sem.at[7], recv_sem.at[7])
    part_q = 3 * width // 6
    qs = [Share(place, ORDERS[p], own_d.at[p], recv_d.at[p], send_sem.at[8 + p], recv_sem.at[8 + p], columns=part_q) for p in range(3)]
    for p in range(3): qs[p].columns = part_q
    r_d = ff // GROUP
    r = width // GROUP
    half_d = r_d // 2

    loads["dy"].wait()
    loads["act"].wait()
    wide = width // 3
    for p in range(3):
        for piece in range(4):
            blocks = GROUP // 4
            val = nn(act[piece * blocks * r_d : (piece + 1) * blocks * r_d, :], dy[:, p * wide : (p + 1) * wide])
            for j in range(blocks):
                v = val[j * r_d : (j + 1) * r_d]
                down[p].store(piece * blocks + j, jnp.concatenate([v[:half_d], v[half_d:]], axis=1))
        down[p].send()
    loads["w_down"].wait()
    loads["slope"].wait()
    step = 768

    def back_act(i, carry):
        at = rows_of(i, step)
        ga = nt(w_down[at, :], dy[...])
        slope[at, :] = (ga * slope[at, :].astype(f32)).astype(bf16)
        return carry

    down[0].pump()
    lax.fori_loop(0, 2, back_act, 0)
    down[1].pump()
    down[2].pump()
    lax.fori_loop(2, ff // step, back_act, 0)
    gp = slope
    loads["h2"].wait()
    half_up = ff // 2
    fold = half_up // 3
    sub = 256
    for p in range(3):
        for q in range(fold // sub):
            at = p * fold + q * sub
            left = nt(h2[...], gp[at : at + sub, :])
            right = nt(h2[...], gp[half_up + at : half_up + at + sub, :])
            for j in range(GROUP):
                v = jnp.concatenate([left[j * r : (j + 1) * r], right[j * r : (j + 1) * r]], axis=0)
                up[p].store(j, v, q * sub)
        up[p].send()
        if p > 0:
            up[p - 1].pump()
    down[0].pump()
    loads["w_up"].wait()
    third = width // 3
    for i in range(3):
        g[i * third : (i + 1) * third, :] = nn(w_up[i * third : (i + 1) * third, :], gp[...])
        if i == 0:
            up[2].pump()
            down[1].pump()
            down[2].pump()
    load("w_qkv", w_qkv_h, w_up.at[:, pl.ds(0, 3 * width)])
    load("w_out", w_out_h, w_up.at[:, pl.ds(3 * width, width)])
    w_qkv = w_up.at[:, pl.ds(0, 3 * width)]
    w_out = w_up.at[:, pl.ds(3 * width, width)]
    loads["after"].wait()

    def keep_after(c, value):
        at = lanes_of(c)
        g[:, at] = value
        da[:, at] = value.astype(bf16)

    norm_back(lambda c: x[:, lanes_of(c)], lambda c: g[:, lanes_of(c)], keep_after, norms[:, 2:3], acc_a, acc_b, chunks,
              lambda c: jnp.transpose(dy[lanes_of(c), :].astype(f32)))
    rows_small[2:3, :] = columns_sum(acc_a)
    rows_small[3:4, :] = columns_sum(acc_b)
    for d in down: d.pump()
    loads["joined"].wait()
    half_o = width // 2
    left = nt(joined[...], da[:half_o, :])
    right = nt(joined[...], da[half_o:, :])
    for j in range(GROUP):
        out.store(j, jnp.concatenate([left[j * r : (j + 1) * r], right[j * r : (j + 1) * r]], axis=0))
    out.send()
    loads["w_out"].wait()
    datt = h2
    datt[...] = nn(w_out[...], da[...]).astype(bf16)
    for d in down: d.pump()
    out.pump()
    loads["qkv"].wait()
    loads["aux"].wait()
    on = flag[0].astype(f32)

    def head_step(h, carry):
        base = pl.multiple_of(h * hd, hd)
        at_q, at_k, at_v = pl.ds(base, hd), pl.ds(width + base, hd), pl.ds(2 * width + base, hd)
        q = qkv[at_q, :seq] * jnp.asarray(scale, bf16)
        k = qkv[at_k, :seq]
        kt = jnp.transpose(k)
        vt = jnp.transpose(qkv[at_v, :seq])
        ks = k * jnp.asarray(scale, bf16)
        do = datt[at_q, :]
        log_total = aux[h, 0:1, :]
        dq, dk, dv = [], [], []
        for first, n in query_blocks(seq):
            keys = first + n
            qb, db = q[:, first:keys], do[:, first:keys]
            s = causal(nn(kt[:keys], qb), first)
            p = jnp.exp(s - log_total[:, first:keys])
            dp = nn(vt[:keys], db)
            ds = (p * (dp - jnp.sum(p * dp, axis=0, keepdims=True))).astype(bf16)
            dq.append(nn(ks[:, :keys], ds))
            dk.append(nt(qb, ds))
            dv.append(nt(db, p.astype(bf16)))
        def add_up(parts):
            total = parts[-1]
            for part in reversed(parts[:-1]):
                have = part.shape[1]
                total = jnp.concatenate([total[:, :have] + part, total[:, have:]], axis=1)
            return total
        dqt, dkt, dvt = jnp.concatenate(dq, axis=1), add_up(dk), add_up(dv)
        sig = aux[h, 1:2, :]
        mk = mem_columns(qkv[at_k, seq:], h)
        mv = mem_columns(qkv[at_v, seq:], h)
        dof = do.astype(f32)
        lane = lax.broadcasted_iota(jnp.int32, (1, seq), 1)
        dgate = on * jnp.sum(dof * by_block(mv, dof.shape, span), axis=0, keepdims=True)
        dscore = dgate * sig * (1.0 - sig) * scale
        dqt = dqt + dscore * by_block(mk, dof.shape, span)
        qf = qkv[at_q, :seq].astype(f32) * dscore
        vf = dof * (sig * on)
        mem_lane = lax.broadcasted_iota(jnp.int32, (hd, LANES), 1)
        def split(wide):
            total = jnp.sum(wide, axis=1, keepdims=True)
            low = jnp.sum(jnp.where(lane < span, wide, 0.0), axis=1, keepdims=True)
            return jnp.where(mem_lane == 2 * h, low, jnp.where(mem_lane == 2 * h + 1, total - low, 0.0)).astype(bf16)
        qkv[at_q, :seq] = dqt.astype(bf16)
        qkv[at_q, seq:] = jnp.zeros((hd, LANES), bf16)
        qkv[at_k, :seq] = dkt.astype(bf16)
        qkv[at_k, seq:] = split(qf)
        qkv[at_v, :seq] = dvt.astype(bf16)
        qkv[at_v, seq:] = split(vf)
        return carry

    quarter = heads // 4
    lax.fori_loop(0, quarter, head_step, 0)
    for d in down: d.pump()
    for u in up: u.pump()
    for p in range(3):
        v = down[p].last()
        s_down[:half_d, p * wide : (p + 1) * wide] = v[:, :wide]
        s_down[half_d:, p * wide : (p + 1) * wide] = v[:, wide:]
    for b in range(STAGES):
        pl.semaphore_signal(ready_sem.at[b], inc=1, device_id=place.partner(b), device_id_type=MESH)
    lax.fori_loop(quarter, 2 * quarter, head_step, 0)
    for u in up: u.pump()
    out.pump()
    lax.fori_loop(2 * quarter, 3 * quarter, head_step, 0)
    for u in up: u.pump()
    out.pump()
    lax.fori_loop(3 * quarter, heads, head_step, 0)
    for u in up: u.pump()
    out.pump()
    loads["h1"].wait()
    for b in range(STAGES):
        pl.semaphore_wait(ready_sem.at[b], 1)
    half_q = 3 * width // 2
    for p in range(3):
        at = p * part_q
        left = nt(h1[...], qkv[at : at + part_q, :])
        right = nt(h1[...], qkv[half_q + at : half_q + at + part_q, :])
        for j in range(GROUP):
            qs[p].store(j, jnp.concatenate([left[j * r : (j + 1) * r], right[j * r : (j + 1) * r]], axis=0))
        qs[p].send()
        if p > 0: qs[p - 1].pump()
    loads["w_qkv"].wait()
    gm = [None] * 3
    for i in range(3):
        val = nn(w_qkv[i * third : (i + 1) * third, :], qkv[...])
        x[i * third : (i + 1) * third, :] = val[:, :seq]
        gm[i] = val[:, seq:]
        if i == 0: qs[2].pump()
    mem_own[...] = jnp.transpose(jnp.concatenate(gm, axis=0))[:32].astype(bf16)
    mem_copy = pltpu.make_async_remote_copy(src_ref=mem_own, dst_ref=mem_recv, send_sem=mem_sem.at[0], recv_sem=mem_sem.at[1],
        device_id=place.beside(), device_id_type=MESH)
    mem_copy.start()
    load("tokens", tokens_h, dy)
    out.pump()
    for p in range(3):
        v = up[p].last()
        s_up[:, p * fold : (p + 1) * fold] = v[:r]
        s_up[:, half_up + p * fold : half_up + (p + 1) * fold] = v[r:]
    v = out.last()
    s_out[:, :half_o] = v[:r]
    s_out[:, half_o:] = v[r:]
    loads["tokens"].wait()

    def keep_tokens(c, value):
        gtok_o[lanes_of(c), :] = jnp.transpose(value)

    norm_back(lambda c: jnp.transpose(dy[lanes_of(c), :].astype(f32)), lambda c: x[:, lanes_of(c)], keep_tokens, norms[:, 0:1],
              acc_a, acc_b, chunks, lambda c: g[:, lanes_of(c)])
    rows_small[0:1, :] = columns_sum(acc_a)
    rows_small[1:2, :] = columns_sum(acc_b)
    rows_small[4:8, :] = jnp.zeros((4, width), f32)
    small_own[0] = rows_small[...]
    small.send()
    load("after2", after_h, x)
    for q in qs: q.pump()
    mem_copy.wait()
    me = place.me_basis
    gcoef_o[me] = tn(weights_e[me], mem_own[...])
    gcoef_o[1 - me] = tn(weights_e[1 - me], mem_recv[...])
    small.pump()
    loads["after2"].wait()
    for i in range(3):
        cols = slice(i * third, (i + 1) * third)
        val = tn(w_down[:, cols], act[...])
        mixed_o[:, cols] = jnp.transpose(x[cols, :] + val).astype(bf16)
        for q in qs:
            if q.stage < STAGES: q.pump()
        small.pump()
    for s in (small,):
        while s.stage < STAGES: s.pump()
    for p in range(3):
        while qs[p].stage < STAGES: qs[p].pump()
        v = qs[p].last()
        s_qkv[:, p * part_q : (p + 1) * part_q] = v[:r]
        s_qkv[:, half_q + p * part_q : half_q + (p + 1) * part_q] = v[r:]
    small_o[...] = small_own[STAGES]


def backward(place, heads, blocks, flag, norms, weights_e, dy, tokens, w_down, w_up, w_out, w_qkv, kept):
    h1, qkv, aux, joined, after, h2, act, slope = kept
    seq, width = dy.shape
    ff = w_up.shape[1]
    span = seq // blocks
    scale = 1.0 / math.sqrt(width // heads)
    r, r_d = width // GROUP, ff // GROUP
    S = jax.ShapeDtypeStruct
    outs = [((seq, width), bf16), ((seq, width), f32), ((2, weights_e.shape[2], width), f32), ((r, 3 * width), f32), ((r, width), f32),
            ((r, ff), f32), ((r_d, width), f32), ((8, width), f32)]
    vm = lambda s, d: pltpu.VMEM(s, d)
    part = ((r_d // 2), 2 * width // 3)
    part_o = (2 * r, width // 2)
    scratch = [vm((seq, width), bf16), vm((ff, seq), bf16), vm((ff, seq), bf16), vm((width, seq), bf16), vm((width, seq), bf16),
        vm(qkv.shape, bf16), vm(aux.shape, f32), vm(h1.shape, bf16), vm(w_down.shape, bf16), vm(w_up.shape, bf16),
        vm((width, seq), f32), vm((width, seq), f32), vm((width, seq), bf16), vm((width, LANES), f32), vm((width, LANES), f32), vm((8, width), f32),
        vm((3, GROUP) + part, bf16), vm((3, GROUP) + part, bf16), vm((GROUP,) + part_o, bf16),
        vm((3, GROUP - 1) + part, bf16), vm((3, GROUP - 1) + part, bf16), vm((GROUP - 1,) + part_o, bf16),
        vm((32, width), bf16), vm((32, width), bf16), vm((STAGES + 1, 8, width), f32), vm((STAGES, 8, width), f32),
        pltpu.SemaphoreType.DMA((15,)), pltpu.SemaphoreType.DMA((4,)), pltpu.SemaphoreType.DMA((11, STAGES)), pltpu.SemaphoreType.DMA((11, STAGES)),
        pltpu.SemaphoreType.REGULAR((STAGES,)), pltpu.SemaphoreType.DMA((2,))]
    return pl.pallas_call(
        functools.partial(backward_kernel, place, heads, span, scale),
        out_shape=[S(*o) for o in outs],
        in_specs=[SM, VM, VM] + [ANY] * 14,
        out_specs=[VM] * len(outs),
        scratch_shapes=scratch,
        compiler_params=pltpu.CompilerParams(vmem_limit_bytes=60 * 2**20, collective_id=0, has_side_effects=True),
    )(flag, norms, weights_e, dy, tokens, act, slope, h2, after, joined, qkv, aux, h1, w_down, w_up, w_out, w_qkv)


def halve_rest(place, rows):
    for bit in reversed(range(place.low)):
        half = rows.shape[0] // 2
        if bit < place.basis_bits:
            axis, size, mask = "basis", place.basis, 1 << bit
        else:
            axis, size, mask = "dp", place.dp, 1 << (bit - place.basis_bits)
        mine = (lax.axis_index(axis) // mask) % 2
        keep = lax.dynamic_slice_in_dim(rows, mine * half, half, 0)
        give = lax.dynamic_slice_in_dim(rows, (1 - mine) * half, half, 0)
        rows = keep + lax.ppermute(give, axis, [(i, i ^ mask) for i in range(size)])
    return rows


def sum_rest(place, values):
    for bit in range(place.low):
        if bit < place.basis_bits:
            axis, size, mask = "basis", place.basis, 1 << bit
        else:
            axis, size, mask = "dp", place.dp, 1 << (bit - place.basis_bits)
        values = values + lax.ppermute(values, axis, [(i, i ^ mask) for i in range(size)])
    return values


def basis_weights(centres, widths, rows):
    spread = (widths * widths).astype(f32) + 4.0
    gap = centres[..., None].astype(f32) - rows.astype(f32)
    return 2.0 * lax.rsqrt(spread)[..., None] * jnp.exp(-gap * gap / (2.0 * spread[..., None]))


def on_device(place, tokens, w_qkv, w_out, w_up, w_down, gain_one, shift_one, gain_two, shift_two, coeffs, flags, centres, widths, cotangent):
    width = tokens.shape[2]
    local = coeffs.shape[1]
    heads, blocks = centres.shape[1], centres.shape[2]
    norms = jnp.stack([gain_one, shift_one, gain_two, shift_two], axis=1)
    rows = lax.axis_index("basis") * local + jnp.arange(local, dtype=jnp.int32)
    weights_e = basis_weights(centres, widths, rows).astype(bf16).reshape(2, heads * blocks, local)
    weights_e = jnp.pad(weights_e, ((0, 0), (0, 32 - heads * blocks), (0, 0)))
    partial_mem = jnp.einsum("srj,sjd->srd", weights_e, coeffs, preferred_element_type=f32)
    me = lax.axis_index("basis")
    give = lax.dynamic_index_in_dim(partial_mem, 1 - me, 0, keepdims=False).astype(bf16)
    keep = lax.dynamic_index_in_dim(partial_mem, me, 0, keepdims=False)
    got = lax.ppermute(give, "basis", [(0, 1), (1, 0)])
    memory = (keep + got.astype(f32)).astype(bf16)
    memory = jnp.pad(memory, ((0, LANES - 32), (0, 0)))
    kept = forward(heads, blocks, flags, tokens[0], norms, memory, w_qkv, w_out, w_up)
    mixed, gtok, gcoef, s_qkv, s_out, s_up, s_down, small = backward(
        place, heads, blocks, flags, norms, weights_e, cotangent[0], tokens[0], w_down, w_up, w_out, w_qkv, kept)
    small = sum_rest(place, small)
    flat = lax.axis_index("dp") * place.basis + lax.axis_index("basis")
    part = width // (place.dp * place.basis)
    small = lax.dynamic_slice_in_dim(small, flat * part, part, 1)
    return (mixed[None], gtok[None], gcoef, *(halve_rest(place, s) for s in (s_qkv, s_out, s_up, s_down)), small[0], small[1], small[2], small[3])


def solution(mesh):
    both = ("dp", "basis")
    in_specs = (P(both, None, None),) + (P(),) * 8 + (P("dp", "basis", None), P(both), P("dp", None, None), P("dp", None, None), P(both, None, None))
    out_specs = (P(both, None, None), P(both, None, None), P("dp", "basis", None)) + (P(both, None),) * 4 + (P(both),) * 4
    return jax.shard_map(functools.partial(on_device, Place(mesh.shape)), mesh=mesh, in_specs=in_specs, out_specs=out_specs, check_vma=False)
```

time: 633 us -> 158 us (0.25)
  waiting for transfers between devices: 354 us -> 0.01 us
  Pallas kernels: 0 us -> 135 us
  matrix products: 123 us -> 0.17 us
  blocking collectives: 47.3 us -> 0 us
  local copies, waits for them, and re-layouts: 56.7 us -> 15.9 us
  other arithmetic: 32.5 us -> 1.55 us
  between operations: 15.5 us -> 1.4 us
    reduce_scatter x5 -> x0, waiting for transfers between devices: 354 us -> none  [the longest x1 142 us: on_device(): lax.psum_scatter(grad_w_up, ('dp', 'basis'), scatter_dimension=0, tiled=T...]
    pallas_call x0 -> x2, Pallas kernels: none -> 135 us  [the longest x1 101 us: backward(): pl.pallas_call(functools.partial(backward_kernel, place, heads, span, sca...]
    dot_general x33 -> x1, matrix products: 123 us -> 0.17 us  [on_device(): jnp.einsum('srj,sjd->srd', weights_e, coeffs, preferred_element_type=f32)]
    unnamed x1 -> x0, blocking collectives: 42.3 us -> none
    convert_element_type x6 -> x4, other arithmetic: 12 us -> 0.85 us  [the longest x2 0.74 us: basis_weights(): gap = centres[..., None].astype(f32) - rows.astype(f32)]
    mul x6 -> x3, local copies, waits for them, and re-layouts: 11 us -> 0.29 us  [the longest x2 0.19 us: basis_weights(): 2.0 * lax.rsqrt(spread)[..., None]]
    another operation x7 -> x5, local copies, waits for them, and re-layouts: 13.7 us -> 3.69 us  [on_device(): norms = jnp.stack([gain_one, shift_one, gain_two, shift_two], axis=1)]
    convert_element_type x4 -> x2, local copies, waits for them, and re-layouts: 9.26 us -> 0.12 us  [the longest x1 0.1 us: basis_weights(): gap = centres[..., None].astype(f32) - rows.astype(f32)]
  transfers between devices with their start and end apart: 5 -> 1, of which waited for: 3 -> 0; matrix products, arithmetic and copies ran while one was open for 23% -> 3% of each run, Pallas kernels for 0% -> 0%
where the time goes in v2:
time: 158 us; the launch traced here: 157 us
  Pallas kernels  135 us (85%)
  local copies, waits for them, and re-layouts  15.9 us (10%)
  starting transfers between devices  3 us (2%)
    pallas_call x1, Pallas kernels, backward(): pl.pallas_call(functools.partial(backward_kernel, place, heads, span, sca...  101 us
    pallas_call x1, Pallas kernels, forward(): pl.pallas_call(functools.partial(forward_kernel, heads, span, scale), out...  34.8 us
    unnamed x19, local copies, waits for them, and re-layouts  8.91 us
    another operation x5, local copies, waits for them, and re-layouts, on_device(): norms = jnp.stack([gain_one, shift_one, gain_two, shift_two], axis=1)  3.69 us
  transfers between devices with their start and end apart: 1, of which 0 were waited for; matrix products, arithmetic and copies ran while one was open for 3% of the time, Pallas kernels for 0%

profile of v2, /device:TPU:0, one launch (start us, length us, event | category | flops | bytes accessed | tf_op | source)
XLA Modules:
  0.0 157.3 jit_solution(17393885074263150559)
XLA Ops:
  0.6 0.0 copy-start
  0.7 0.7 convert_element_type.35
  1.4 0.7 rsqrt_multiply_fusion
  2.1 0.1 copy.35
  2.2 0.1 mul.37
  2.3 0.1 copy.36
  2.4 0.1 sub.19
  2.5 0.1 copy.37
  2.6 0.1 div.11
  2.7 0.1 fusion.5
  2.8 0.0 copy-done
  2.8 0.2 fusion.7
  3.0 3.0 %collective-permute-start = (bf16[32,768]{1,0:T(8,128)(2,1)S(1)}, bf16[32,768]{1,0:T(8,128)(2,1)S(1)}, u32[]{:S(2)}, u32[]{:S(2)}) collective-permute-start(bf16[32,768]{1,0:T(8,128)(2,1)S(1)} %fusion.1), channel_id=1, source_target_pairs={{0,1},{1,0},{2,3},{3,2},{4,5},{5,4},{6,7},{7,6},{8,9},{9,8},{10,11... | collective-permute-start | bytes 147464 | tf_op jit(solution)/shard_map/ppermute | solution.py:638
  6.0 0.7 stack.15
  6.7 0.7 stack.16
  7.4 0.7 stack.17
  8.1 0.7 stack.18
  9.4 0.6 pad.8.weights_e
  10.0 0.9 copy.39.norms
  11.0 0.0 collective-permute-done
  11.0 0.7 pad.9.memory
  11.7 34.8 %shard_map.221 = (bf16[768,768]{1,0:T(8,128)(2,1)}, bf16[2304,768]{1,0:T(8,128)(2,1)}, f32[12,8,640]{2,1,0:T(8,128)}, bf16[768,640]{1,0:T(8,128)(2,1)}, f32[768,...) custom-call(s32[1]{0:T(128)S(6)} %copy.47.flag, ...), custom_call_target="tpu_custom_call" | custom-call | tf_op jit(solution)/shard_map/pallas_call | solution.py:150
  46.5 100.5 %shard_map.222 = (bf16[640,768]{1,0:T(8,128)(2,1)}, f32[640,768]{1,0:T(8,128)}, f32[2,128,768]{2,1,0:T(8,128)}, f32[24,2304]{1,0:T(8,128)}, f32[24,768]{1,0:T(8,...) custom-call(s32[1]{0:T(128)S(6)} %copy.47.flag, f32[768,4]{1,0:T(8,128)} %copy.39.norms, ...), custom_call_target="tpu_custom_call" | custom-call | tf_op jit(solution)/shard_map/pallas_call | solution.py:586
  147.0 0.0 copy-start.1
  147.0 0.8 constant_dynamic-slice_fusion
  147.9 0.5 slice_bitcast_fusion
  148.4 0.0 copy-start.4
  148.4 0.0 copy-start.5
  148.4 2.3 %copy.48 = bf16[1,640,768]{2,1,0:T(8,128)(2,1)} copy(bf16[1,640,768]{2,1,0:T(8,128)(2,1)} %bitcast.23) | data formatting | bytes 1966080
  150.7 0.0 copy-start.3
  150.7 0.0 copy-start.2
  150.7 3.0 %copy.49 = f32[1,640,768]{2,1,0:T(8,128)} copy(f32[1,640,768]{2,1,0:T(8,128)} %bitcast.21) | data formatting | bytes 3932160
  153.7 0.0 copy-done.1
  153.7 0.9 copy.50
  154.6 0.0 copy-done.4
  154.6 0.7 copy.51
  155.3 0.0 copy-done.5
  155.3 0.6 copy.52
  155.9 0.0 copy-done.3
  155.9 0.7 copy.53
  156.6 0.0 copy-done.2
  156.6 0.7 copy.54
  (4 shorter events, 0.1 us)
Async XLA Ops:
  0.6 2.1 %copy-start = (bf16[2,128,768]{2,1,0:T(8,128)(2,1)S(1)}, bf16[2,128,768]{2,1,0:T(8,128)(2,1)}, u32[]{:S(2)}) copy-start(bf16[2,128,768]{2,1,0:T(8,128)(2,1)} %param.23) | copy-start | bytes 1179652
  3.0 8.0 %collective-permute-start = (bf16[32,768]{1,0:T(8,128)(2,1)S(1)}, bf16[32,768]{1,0:T(8,128)(2,1)S(1)}, u32[]{:S(2)}, u32[]{:S(2)}) collective-permute-start(bf16[32,768]{1,0:T(8,128)(2,1)S(1)} %fusion.1), channel_id=1, source_target_pairs={{0,1},{1,0},{2,3},{3,2},{4,5},{5,4},{6,7},{7,6},{8,9},{9,8},{10,11... | collective-permute-start | bytes 147464 | tf_op jit(solution)/shard_map/ppermute | solution.py:638
  147.0 6.7 %copy-start.1 = (f32[2,128,768]{2,1,0:T(8,128)S(1)}, f32[2,128,768]{2,1,0:T(8,128)}, u32[]{:S(2)}) copy-start(f32[2,128,768]{2,1,0:T(8,128)} %get-tuple-element.62) | copy-start | bytes 2359300
  148.4 6.2 %copy-start.4 = (f32[24,2304]{1,0:T(8,128)S(1)}, f32[24,2304]{1,0:T(8,128)}, u32[]{:S(2)}) copy-start(f32[24,2304]{1,0:T(8,128)} %get-tuple-element.63) | copy-start | bytes 663556
  148.4 6.8 %copy-start.5 = (f32[24,768]{1,0:T(8,128)S(1)}, f32[24,768]{1,0:T(8,128)}, u32[]{:S(2)}) copy-start(f32[24,768]{1,0:T(8,128)} %get-tuple-element.64) | copy-start | bytes 221188
  150.7 5.2 %copy-start.3 = (f32[24,3072]{1,0:T(8,128)S(1)}, f32[24,3072]{1,0:T(8,128)}, u32[]{:S(2)}) copy-start(f32[24,3072]{1,0:T(8,128)} %get-tuple-element.65) | copy-start | bytes 884740
  150.7 5.9 %copy-start.2 = (f32[96,768]{1,0:T(8,128)S(1)}, f32[96,768]{1,0:T(8,128)}, u32[]{:S(2)}) copy-start(f32[96,768]{1,0:T(8,128)} %get-tuple-element.66) | copy-start | bytes 884740
